TPU v7x, 512 devices: a whole 4x4x16 slice. The times are simulated.
512 devices in a mesh: cuts: 16 (over y, x_hi, core), idx: 32 (over z, x_lo).
Axes of the slice: x: 4 (x_hi: 2, x_lo: 2; x = x_hi * 2 + x_lo), y: 4, z: 16, core: 2. Of those that a mesh axis runs over, the one named last changes fastest.
Arguments:
- boundary: bfloat16 [2, 16, 4194304], P(None, 'cuts', 'idx'), may hold values from -1.5 to 1.5
- gates_shared: bfloat16 [2, 2, 256, 256], replicated, may hold values from -0.25 to 0.25
- gates_sliced: bfloat16 [2, 16, 256, 256], P(None, 'cuts'), may hold values from -0.25 to 0.25
- cotangent: bfloat16 [2, 32, 256, 512], P(None, 'idx', 'cuts'), may hold values from -0.03125 to 0.03125
Outputs:
- amplitudes: float32 [2, 32, 256, 512], P(None, 'idx', 'cuts')
- grad_shared: float32 [2, 2, 256, 256], P(None, None, 'cuts')
- grad_sliced: float32 [2, 16, 256, 256], P(None, 'cuts')
All inputs are finite; a program needn't handle non-finite values.
Results may differ from a plain program's by a relative error of at most 0.0042.
Values may be sent and summed in bfloat16 or wider, within the bound.
A program may use at most 64 MiB of HBM per device.

v0:
```python
import jax
import jax.numpy as jnp
from jax import lax
from jax.sharding import PartitionSpec as P

RANK = 22
SHARED = 8
MIDDLE = 5


def gate_apply(formula, tensor, gate, conjugate):
    gate_real = gate[0]
    gate_imag = -gate[1] if conjugate else gate[1]
    real_part = jnp.einsum(
        formula, tensor[0], gate_real, preferred_element_type=jnp.float32
    ) - jnp.einsum(formula, tensor[1], gate_imag, preferred_element_type=jnp.float32)
    imag_part = jnp.einsum(
        formula, tensor[1], gate_real, preferred_element_type=jnp.float32
    ) + jnp.einsum(formula, tensor[0], gate_imag, preferred_element_type=jnp.float32)
    return jnp.stack([real_part, imag_part])


def grad_prod(formula, tensor, cotan):
    real_part = jnp.einsum(
        formula, tensor[0], cotan[0], preferred_element_type=jnp.float32
    ) + jnp.einsum(formula, tensor[1], cotan[1], preferred_element_type=jnp.float32)
    imag_part = jnp.einsum(
        formula, tensor[0], cotan[1], preferred_element_type=jnp.float32
    ) - jnp.einsum(formula, tensor[1], cotan[0], preferred_element_type=jnp.float32)
    return jnp.stack([real_part, imag_part])


def local(boundary, gates_shared, gates_sliced, cotangent):
    idx_count = lax.axis_size("idx")
    dist_bits = idx_count.bit_length() - 1
    slice_count = boundary.shape[1]
    width = 2**SHARED
    size_b = 2 ** (SHARED - dist_bits)
    size_c1 = 2**MIDDLE
    size_c2 = 2 ** (RANK - 2 * SHARED - MIDDLE)
    size_e2 = 2 ** (MIDDLE - dist_bits)
    size_d = 2 ** (SHARED - MIDDLE)
    size_f = size_e2 * size_d
    row_count = size_b * size_c1 * size_c2
    whole_cot = lax.all_gather(cotangent, "cuts", axis=2, tiled=True)
    start_tensor = boundary.reshape(2, slice_count, row_count, width)
    gate_one = gates_shared[0].reshape(2, width, idx_count, size_f)
    gate_two = gates_shared[1].reshape(2, idx_count, size_b, width)
    gate_three = gates_sliced.reshape(2, slice_count, size_c1, size_d, size_c1, size_d)
    first_tensor = gate_apply("lmu,uef->lfem", start_tensor, gate_one, False).astype(jnp.bfloat16)
    pieces = lax.all_to_all(first_tensor, "idx", split_axis=3, concat_axis=3, tiled=True)
    items = pieces.shape[2]
    viewed = pieces.reshape(2, slice_count, items, idx_count, size_b, size_c1 * size_c2)
    result = gate_apply("lfabk,abs->lfks", viewed, gate_two, False).astype(jnp.bfloat16)
    second_view = result.reshape(2, slice_count, size_e2, size_d, size_c1, size_c2, width)
    third_tensor = gate_apply("lgdcjs,lcdxe->lsxjge", second_view, gate_three, False)
    local_amp = jnp.sum(third_tensor, axis=1).reshape(2, 1, width, -1)
    amplitudes = lax.psum_scatter(local_amp, "cuts", scatter_dimension=2, tiled=True)
    cot_view = whole_cot.reshape(2, width, size_c1, size_c2, size_e2, size_d)
    grad_three = grad_prod("lgdcjs,sxjge->lcdxe", second_view, cot_view).reshape(
        2, slice_count, width, width
    )
    back_two = gate_apply("sxjge,lcdxe->lgdcjs", cot_view, gate_three, True).astype(jnp.bfloat16)
    back_two = back_two.reshape(2, slice_count, size_f, size_c1 * size_c2, width)
    first_view = pieces.reshape(2, slice_count, size_f, idx_count, size_b, size_c1 * size_c2)
    grad_two = grad_prod("lfabk,lfks->abs", first_view, back_two).reshape(2, width, width)
    back_one = gate_apply("lfks,abs->lfabk", back_two, gate_two, True).astype(jnp.bfloat16)
    back_one = back_one.reshape(2, slice_count, size_f, idx_count, row_count)
    returned = lax.all_to_all(back_one, "idx", split_axis=3, concat_axis=3, tiled=True)
    grad_one = grad_prod("lmu,lfem->uef", start_tensor, returned).reshape(2, width, width)
    shared_terms = jnp.stack([grad_one, grad_two])
    totals, sliced_grad = lax.psum((shared_terms, grad_three), "idx")
    shared_grad = lax.psum_scatter(totals, "cuts", scatter_dimension=2, tiled=True)
    return (amplitudes, shared_grad, sliced_grad)


def solution(mesh):
    placed = (
        P(None, "cuts", "idx"),
        P(),
        P(None, "cuts", None, None),
        P(None, "idx", "cuts", None),
    )
    return jax.shard_map(
        local,
        mesh=mesh,
        in_specs=placed,
        out_specs=(
            P(None, "idx", "cuts", None),
            P(None, None, "cuts", None),
            P(None, "cuts", None, None),
        ),
        check_vma=False,
    )
```

profile of v0, /device:TPU:16, one launch (start us, length us, event | category | flops | bytes accessed | tf_op | source)
XLA Modules:
  0.0 560.5 jit_solution(8721317619409511983)
XLA Ops:
  7.2 4.1 slice_reduce_fusion.1
  11.4 0.7 negate_bitcast_fusion
  13.6 0.9 copy.97
  14.5 16.5 %all-to-all-start = ((bf16[2,1,8,32,512]{4,2,1,0,3:T(8,128)(2,1)}), bf16[2,1,8,32,512]{4,2,1,0,3:T(8,128)(2,1)}, u32[]{:S(2)}, u32[]{:S(2)}) async-start(bf16[2,1,8,32,512]{4,2,1,0,3:T(8,128)(2,1)} %copy.97), calls=%async_computation | async-start | bytes 1048576 | tf_op jit(solution)/shard_map/all_to_all | solution.py:51
  31.0 0.7 fusion.117
  31.7 2.5 reshape.414
  34.2 3.2 copy.103
  37.3 1.6 copy.115
  38.9 3.4 reshape.412
  42.3 3.2 copy.101
  45.5 22.6 %all_gather.3 = bf16[2,1,256,512]{3,0,1,2:T(2,128)(2,1)S(1)} all-gather(bf16[2,1,16,512]{3,0,1,2:T(2,128)(2,1)S(1)} %copy.111), channel_id=1, replica_groups=mesh['cuts'=16,'idx'=32] {'cuts'}, dimensions={2}, use_global_device_ids=true | all-gather | bytes 557056 | tf_op jit(solution)/shard_map/all_gather | solution.py:45
  68.1 1.5 fusion.115
  69.6 0.5 copy.235
  70.1 1.3 copy.234
  71.4 1.5 convolution_bitcast_fusion.5
  73.0 1.4 convolution_bitcast_fusion.4
  74.4 1.3 fusion.33
  75.7 0.3 fusion.84
  76.1 1.3 fusion.30
  77.4 0.3 fusion.16
  78.0 0.3 stack.70
  78.3 0.3 fusion.90
  78.6 0.3 fusion.17
  79.2 0.3 stack.69
  79.6 1.1 copy.131
  80.7 12.2 %all-to-all-start.1 = ((bf16[2,1,8,32,512]{4,2,1,0,3:T(8,128)(2,1)}), bf16[2,1,8,32,512]{4,2,1,0,3:T(8,128)(2,1)}, u32[]{:S(2)}, u32[]{:S(2)}) async-start(bf16[2,1,8,32,512]{4,2,1,0,3:T(8,128)(2,1)} %copy.131), calls=%async_computation.1 | async-start | bytes 1048576 | tf_op jit(solution)/shard_map/all_to_all | solution.py:69
  93.1 1.1 fusion.116
  94.6 0.3 convolution_bitcast_fusion.12
  95.3 1.0 fusion.37
  96.3 1.1 reshape.411
  97.4 0.3 convolution_bitcast_fusion.9
  97.7 0.3 fusion.36
  98.2 1.4 convolution_bitcast_fusion.6
  99.7 1.4 fusion.29
  101.1 0.3 copy.109
  101.4 0.3 convolution_bitcast_fusion.8
  101.7 0.3 fusion.27
  102.0 0.3 copy.104
  102.4 1.3 copy.110
  103.7 0.3 convolution_bitcast_fusion.14
  104.0 0.3 fusion.47
  104.5 0.3 convolution_bitcast_fusion.16
  104.8 0.3 fusion.45
  105.2 21.1 %all-to-all-done.1 = bf16[2,1,8,32,512]{4,2,1,0,3:T(8,128)(2,1)} async-done(((bf16[2,1,8,32,512]{4,2,1,0,3:T(8,128)(2,1)}), bf16[2,1,8,32,512]{4,2,1,0,3:T(8,128)(2,1)}, u32[]{:S(2)}, u32[]{:S(2)}) %all-to-all-start.1) | async-done | bytes 524320 | tf_op jit(solution)/shard_map/all_to_all | solution.py:69
  126.3 1.1 fusion.114
  128.4 0.3 copy_bitcast_fusion.2
  128.8 1.4 copy.146
  130.2 1.3 dynamic-slice
  132.2 0.5 convolution_bitcast_fusion
  132.6 0.5 fusion.7
  133.1 2.7 copy.156
  135.8 4.0 stack.80
  139.8 0.5 convolution_bitcast_fusion.2
  140.3 0.5 fusion.5
  140.8 2.7 copy.151
  143.5 4.0 stack.79
  147.5 0.8 pad_maximum_fusion.3
  148.3 126.8 %all-reduce.9.cloned.1.call-done = (f32[2,1,256,512]{3,0,1,2:T(2,128)}, f32[2,2,256,256]{3,1,0,2:T(2,128)}) async-done(((f32[2,1,256,512]{3,0,1,2:T(2,128)}, f32[2,2,256,256]{3,1,0,2:T(2,128)}), (f32[2,1,256,512]{3,0,1,2:T(2,128)}, f32[2,2,256,256]{3,1,0,2:T(2,128)})) %all-reduce.9.cloned.1.call-update) | async-done | bytes 2097168
  275.1 1.5 constant_dynamic-slice_fusion
  276.6 0.9 constant_dynamic-slice_fusion.1
  277.4 0.6 copy.157
  278.1 272.3 %all-reduce.7.cloned.1.call-done = (f32[2,2,16,256]{3,1,0,2:T(2,128)}, f32[2,1,256,256]{3,2,1,0:T(8,128)}) async-done(((f32[2,2,16,256]{3,1,0,2:T(2,128)}, f32[2,1,256,256]{3,2,1,0:T(8,128)}), (f32[2,2,16,256]{3,1,0,2:T(2,128)}, f32[2,1,256,256]{3,2,1,0:T(8,128)})) %all-reduce.7.cloned.1.call-update) | async-done | bytes 589840 | tf_op jit(solution)/shard_map/psum | solution.py:72
  550.4 1.5 copy.158
  551.8 1.9 copy.346
  (59 shorter events, 4.6 us)
Async XLA Ops:
  7.2 4.3 copy-start.6
  13.2 17.8 %copy-start.12 = (bf16[2,1,256,256]{3,2,1,0:T(8,128)(2,1)S(1)}, bf16[2,1,256,256]{3,2,1,0:T(8,128)(2,1)}, u32[]{:S(2)}) copy-start(bf16[2,1,256,256]{3,2,1,0:T(8,128)(2,1)} %param.6) | copy-start | bytes 786436
  14.5 66.2 %all-to-all-start = ((bf16[2,1,8,32,512]{4,2,1,0,3:T(8,128)(2,1)}), bf16[2,1,8,32,512]{4,2,1,0,3:T(8,128)(2,1)}, u32[]{:S(2)}, u32[]{:S(2)}) async-start(bf16[2,1,8,32,512]{4,2,1,0,3:T(8,128)(2,1)} %copy.97), calls=%async_computation | async-start | bytes 1048576 | tf_op jit(solution)/shard_map/all_to_all | solution.py:51
  38.9 6.6 %copy-start.13 = (bf16[2,1,16,512]{3,2,1,0:T(8,128)(2,1)S(1)}, bf16[2,1,16,512]{3,2,1,0:T(8,128)(2,1)}, u32[]{:S(2)}) copy-start(bf16[2,1,16,512]{3,2,1,0:T(8,128)(2,1)} %param.7) | copy-start | bytes 98308
  70.1 4.4 copy-start
  71.4 4.7 copy-start.2
  76.1 1.3 copy-start.8
  77.7 0.9 copy-start.9
  79.6 15.0 %copy-start.7 = (bf16[2,2,256,256]{3,2,1,0:T(8,128)(2,1)S(1)}, bf16[2,2,256,256]{3,2,1,0:T(8,128)(2,1)}, u32[]{:S(2)}) copy-start(bf16[2,2,256,256]{3,2,1,0:T(8,128)(2,1)} %param.5) | copy-start | bytes 1572868
  80.7 45.6 %all-to-all-start.1 = ((bf16[2,1,8,32,512]{4,2,1,0,3:T(8,128)(2,1)}), bf16[2,1,8,32,512]{4,2,1,0,3:T(8,128)(2,1)}, u32[]{:S(2)}, u32[]{:S(2)}) async-start(bf16[2,1,8,32,512]{4,2,1,0,3:T(8,128)(2,1)} %copy.131), calls=%async_computation.1 | async-start | bytes 1048576 | tf_op jit(solution)/shard_map/all_to_all | solution.py:69
  92.9 182.2 %all-reduce.9.cloned.1.call-start = ((), (), s32[]{:S(2)}) async-start(), calls=%async_computation.3 | async-start | bytes 4194304
  98.2 3.2 copy-start.4
  98.2 3.2 copy-start.10
  99.6 2.1 copy-start.11
  128.8 3.4 copy-start.3
  128.8 3.4 copy-start.5
  130.1 2.5 copy-start.1
  130.2 420.2 %all-reduce.7.cloned.1.call-start = ((), (), s32[]{:S(2)}) async-start(), calls=%async_computation.2 | async-start | bytes 1179648 | tf_op jit(solution)/shard_map/psum | solution.py:72
Sparse Core Ops, SparseCore 0:
  130.3 144.7 all-reduce.8
  278.6 271.6 all-reduce.6
where the time goes:
time: 562 us; the launch traced here: 561 us
  waiting for transfers between devices  420 us (75%)
  local copies, waits for them, and re-layouts  54.3 us (10%)
  starting transfers between devices  29 us (5%)
  blocking collectives  22.6 us (4%)
  matrix products  17.5 us (3%)
  between operations  15.3 us (3%)
    psum x1, waiting for transfers between devices, local(): totals, sliced_grad = lax.psum((shared_terms, grad_three), 'idx')  272 us
    unnamed x3, waiting for transfers between devices  127 us
    all_gather x1, blocking collectives, local(): whole_cot = lax.all_gather(cotangent, 'cuts', axis=2, tiled=True)  22.6 us
    all_to_all x1, waiting for transfers between devices, local(): lax.all_to_all(back_one, 'idx', split_axis=3, concat_axis=3, tiled=True)  21.1 us
    all_to_all x1, starting transfers between devices, local(): lax.all_to_all(first_tensor, 'idx', split_axis=3, concat_axis=3, tiled=True)  16.5 us
    another operation x11, local copies, waits for them, and re-layouts  15.6 us
    all_to_all x1, starting transfers between devices, local(): lax.all_to_all(back_one, 'idx', split_axis=3, concat_axis=3, tiled=True)  12.2 us
  transfers between devices with their start and end apart: 4, of which 3 were waited for; matrix products, arithmetic and copies ran while one was open for 10% of the time, Pallas kernels for 0%

commit v1 on v0

v1 whole, which is shorter than its diff:
```python
import jax
import jax.numpy as jnp
from jax import lax
from jax.sharding import PartitionSpec as P


def cdot(formula, left, right, conj_left=False, conj_right=False):
    def one(a, b):
        return jnp.einsum(formula, left[a], right[b], preferred_element_type=jnp.float32)

    sl = -1.0 if conj_left else 1.0
    sr = -1.0 if conj_right else 1.0
    real = one(0, 0) - (sl * sr) * one(1, 1)
    imag = sr * one(0, 1) + sl * one(1, 0)
    return jnp.stack([real, imag])


def local(boundary, gates_shared, gates_sliced, cotangent):
    bf = jnp.bfloat16
    start = boundary.reshape(2, 8, 32, 2, 256)
    w1 = gates_shared[0].reshape(2, 256, 32, 8)
    w2 = gates_shared[1]
    w3 = gates_sliced.reshape(2, 32, 8, 32, 8)
    g3 = lax.all_to_all(cotangent[:, 0], "cuts", split_axis=2, concat_axis=1, tiled=True)
    g3b = cdot("vq,uv->uq", g3, w2, conj_right=True).astype(bf)
    g3b = g3b.reshape(2, 32, 8, 32)
    g3b = lax.all_to_all(g3b, "idx", split_axis=1, concat_axis=1, tiled=True)
    g3b = lax.all_gather(g3b, "cuts", axis=3, tiled=True)
    g3b = g3b.reshape(2, 32, 8, 32, 2, 8)
    first = cdot("lckm,med->lcked", start, w1).astype(bf)
    third = cdot("lcked,cdxy->xkyle", first, w3)
    total = lax.psum_scatter(third, "cuts", scatter_dimension=1, tiled=True).astype(bf)
    total = lax.all_to_all(total, "idx", split_axis=5, concat_axis=5, tiled=True)
    total = total.reshape(2, 32, 8, 32)
    total = total.transpose(0, 3, 2, 1).reshape(2, 256, 32)
    part = cdot("uq,uv->vq", total, w2)
    amp = lax.all_to_all(part, "cuts", split_axis=1, concat_axis=2, tiled=True)
    grad_two = cdot("uq,vq->uv", total, g3, conj_left=True)
    grad_three = cdot("lcked,elxky->cdxy", first, g3b, conj_left=True).reshape(2, 1, 256, 256)
    back_one = cdot("elxky,cdxy->lcked", g3b, w3, conj_right=True).astype(bf)
    grad_one = cdot("lckm,lcked->med", start, back_one, conj_left=True).reshape(2, 256, 256)
    shared = jnp.stack([grad_one, grad_two], axis=0)
    shared = lax.psum_scatter(shared, "cuts", scatter_dimension=2, tiled=True)
    shared, sliced = lax.psum((shared, grad_three), "idx")
    return amp[:, None], shared, sliced


def solution(mesh):
    return jax.shard_map(
        local,
        mesh=mesh,
        in_specs=(
            P(None, "cuts", "idx"),
            P(),
            P(None, "cuts", None, None),
            P(None, "idx", "cuts", None),
        ),
        out_specs=(
            P(None, "idx", "cuts", None),
            P(None, None, "cuts", None),
            P(None, "cuts", None, None),
        ),
        check_vma=False,
    )
```

time: 562 us -> 580 us (1.032)
  the two profiles are of different devices: /device:TPU:16 before, /device:TPU:4 now
where the time goes in v1:
time: 580 us; the launch traced here: 578 us
  waiting for transfers between devices  367 us (63%)
  local copies, waits for them, and re-layouts  70.1 us (12%)
  blocking collectives  42 us (7%)
  starting transfers between devices  37.3 us (6%)
  matrix products  33.9 us (6%)
  between operations  14.3 us (2%)
  other arithmetic  13.2 us (2%)
    psum x1, waiting for transfers between devices, local(): shared, sliced = lax.psum((shared, grad_three), 'idx')  252 us
    reduce_scatter x1, waiting for transfers between devices, local(): shared = lax.psum_scatter(shared, 'cuts', scatter_dimension=2, tiled=True)  60.4 us
    reduce_scatter x1, waiting for transfers between devices, local(): lax.psum_scatter(third, 'cuts', scatter_dimension=1, tiled=True).astype(bf)  45 us
    dot_general x32, matrix products, one(): jnp.einsum(formula, left[a], right[b], preferred_element_type=jnp.float32)  33.9 us
    all_gather x1, blocking collectives, local(): g3b = lax.all_gather(g3b, 'cuts', axis=3, tiled=True)  31.6 us
    squeeze x6, local copies, waits for them, and re-layouts, one(): right[b]  16.6 us
    another operation x6, local copies, waits for them, and re-layouts, cdot(): return jnp.stack([real, imag])  15.7 us
    all_to_all x1, starting transfers between devices, local(): g3b = lax.all_to_all(g3b, 'idx', split_axis=1, concat_axis=1, tiled=True)  13.9 us
  transfers between devices with their start and end apart: 6, of which 4 were waited for; matrix products, arithmetic and copies ran while one was open for 16% of the time, Pallas kernels for 0%

profile of v1, /device:TPU:4, one launch (start us, length us, event | category | flops | bytes accessed | tf_op | source)
XLA Modules:
  0.0 578.3 jit_solution(2412485941156705348)
XLA Ops:
  7.2 1.0 copy.229
  8.4 0.9 reshape.121
  9.3 9.8 %all-to-all-start.2 = ((bf16[16,2,512]{2,1,0:T(2,128)(2,1)}), bf16[16,2,512]{2,1,0:T(2,128)(2,1)}, u32[]{:S(2)}, u32[]{:S(2)}) async-start(bf16[16,2,512]{2,1,0:T(2,128)(2,1)} %reshape.121), calls=%async_computation.3 | async-start | bytes 65536 | tf_op jit(solution)/shard_map/all_to_all | solution.py:24
  19.0 4.1 slice_reduce_fusion
  24.5 2.5 squeeze.39
  26.9 2.0 copy.273
  29.8 1.4 subtract_convert_fusion
  31.7 4.3 squeeze.41
  36.1 3.0 copy.280
  39.1 2.1 fusion.26
  41.8 1.9 fusion.4
  43.7 1.9 fusion.3
  45.6 1.7 reshape.122
  47.3 1.8 copy.230
  49.1 0.9 fusion.88
  49.9 1.1 fusion.58
  51.0 1.7 convolution_multiply_fusion.2
  52.8 1.1 fusion.20
  54.6 1.1 fusion.21
  56.4 1.6 copy_bitcast_fusion.2
  58.0 1.7 reshape.123
  59.7 13.9 %all-to-all-start.3 = ((bf16[32,2,256]{2,1,0:T(2,128)(2,1)}), bf16[32,2,256]{2,1,0:T(2,128)(2,1)}, u32[]{:S(2)}, u32[]{:S(2)}) async-start(bf16[32,2,256]{2,1,0:T(2,128)(2,1)} %reshape.123), calls=%async_computation.4 | async-start | bytes 65536 | tf_op jit(solution)/shard_map/all_to_all | solution.py:27
  73.6 5.0 pad_maximum_fusion
  78.7 6.4 %copy.221 = f32[2,32,2,8,8,32]{5,4,3,2,0,1:T(8,128)} copy(f32[2,32,2,8,8,32]{1,5,3,2,4,0:T(8,128)} %pad_maximum_fusion) | data formatting | bytes 2097152 | tf_op jit(solution)/shard_map/stack | solution.py:15
  85.1 1.9 copy.289
  87.0 3.0 copy.292
  89.9 0.9 reshape.124
  91.1 31.6 %all_gather.3 = bf16[2,32,8,512]{1,2,0,3:T(8,128)(2,1)S(1)} all-gather(bf16[2,32,8,32]{1,2,0,3:T(8,128)(2,1)S(1)} %copy.234), channel_id=1, replica_groups=mesh['cuts'=16,'idx'=32] {'cuts'}, dimensions={3}, use_global_device_ids=true | all-gather | bytes 557056 | tf_op jit(solution)/shard_map/all_gather | solution.py:28
  122.9 1.7 copy.291
  124.7 1.7 copy.312
  126.5 1.0 copy.288
  127.5 1.7 copy.309
  129.3 2.4 fusion.90
  131.7 1.3 fusion.91
  133.0 1.3 fusion.5
  134.3 0.8 convolution_bitcast_fusion.3
  135.7 1.3 fusion.6
  137.0 1.5 convolution_bitcast_fusion.1
  138.5 1.5 fusion.15
  140.0 1.8 fusion.32
  141.8 1.8 fusion.36
  143.5 45.0 %reduce-scatter.3.cloned.1.call-done = f32[2,2,2,8,8,32]{5,4,3,2,0,1:T(8,128)} async-done(((f32[2,32,2,8,8,32]{5,4,3,2,0,1:T(8,128)}), f32[2,2,2,8,8,32]{5,4,3,2,0,1:T(8,128)}) %reduce-scatter.3.cloned.1.call-update) | async-done | bytes 65552 | tf_op jit(solution)/shard_map/reduce_scatter | solution.py:32
  188.5 1.0 convert_element_type.3
  189.5 0.9 copy.222
  190.4 1.2 reshape.117
  191.6 13.2 %all-to-all-start = ((bf16[32,2,256]{2,1,0:T(2,128)(2,1)}), bf16[32,2,256]{2,1,0:T(2,128)(2,1)S(1)}, u32[]{:S(2)}, u32[]{:S(2)}) async-start(bf16[32,2,256]{2,1,0:T(2,128)(2,1)} %reshape.117), calls=%async_computation.1 | async-start | bytes 65536 | tf_op jit(solution)/shard_map/all_to_all | solution.py:33
  205.1 2.0 fusion.16
  207.6 0.8 copy.256
  208.4 9.8 %all-to-all-done = bf16[32,2,256]{2,1,0:T(2,128)(2,1)S(1)} async-done(((bf16[32,2,256]{2,1,0:T(2,128)(2,1)}), bf16[32,2,256]{2,1,0:T(2,128)(2,1)S(1)}, u32[]{:S(2)}, u32[]{:S(2)}) %all-to-all-start) | async-done | bytes 32800 | tf_op jit(solution)/shard_map/all_to_all | solution.py:33
  220.6 2.0 pad_maximum_fusion.1
  222.7 1.8 fusion.29
  224.4 2.7 copy.261
  227.1 4.0 stack.89
  231.2 2.1 fusion.30
  234.2 2.7 copy.266
  236.9 4.1 stack.90
  241.0 0.8 pad_maximum_fusion.2
  242.0 60.4 %reduce-scatter.5.cloned.1.call-done = f32[2,2,16,256]{3,2,1,0:T(8,128)} async-done(((f32[2,2,256,256]{3,2,1,0:T(8,128)}), f32[2,2,16,256]{3,2,1,0:T(8,128)}) %reduce-scatter.5.cloned.1.call-update) | async-done | bytes 65552 | tf_op jit(solution)/shard_map/reduce_scatter | solution.py:43
  303.5 10.4 %all_to_all.40 = f32[16,1,1024]{2,1,0:T(1,128)S(1)} all-to-all(f32[16,1,1024]{2,1,0:T(1,128)S(1)} %reshape.119), channel_id=1, replica_groups=mesh['cuts'=16,'idx'=32] {'cuts'}, dimensions={0} | all-to-all | bytes 131072 | tf_op jit(solution)/shard_map/all_to_all | solution.py:37
  314.4 0.8 reduce.4
  315.5 0.8 broadcast_in_dim.3
  316.3 252.2 %all-reduce.3.cloned.1.call-done = (f32[2,2,16,256]{3,2,1,0:T(8,128)}, f32[2,1,256,256]{3,2,1,0:T(8,128)}) async-done(((f32[2,2,16,256]{3,2,1,0:T(8,128)}, f32[2,1,256,256]{3,2,1,0:T(8,128)}), (f32[2,2,16,256]{3,2,1,0:T(8,128)}, f32[2,1,256,256]{3,2,1,0:T(8,128)})) %all-reduce.3.cloned.1.call-update) | async-done | bytes 589840 | tf_op jit(solution)/shard_map/psum | solution.py:44
  568.5 1.5 copy.447
  569.9 1.9 copy.448
  (85 shorter events, 12.2 us)
Async XLA Ops:
  7.2 16.2 %copy-start.4 = (bf16[2,2,256,256]{3,2,1,0:T(8,128)(2,1)S(1)}, bf16[2,2,256,256]{3,2,1,0:T(8,128)(2,1)}, u32[]{:S(2)}) copy-start(bf16[2,2,256,256]{3,2,1,0:T(8,128)(2,1)} %param.5) | copy-start | bytes 1572868
  8.3 15.4 %copy-start.14 = (bf16[2,1,256,256]{3,2,1,0:T(8,128)(2,1)S(1)}, bf16[2,1,256,256]{3,2,1,0:T(8,128)(2,1)}, u32[]{:S(2)}) copy-start(bf16[2,1,256,256]{3,2,1,0:T(8,128)(2,1)} %param.6) | copy-start | bytes 786436
  9.3 36.3 %all-to-all-start.2 = ((bf16[16,2,512]{2,1,0:T(2,128)(2,1)}), bf16[16,2,512]{2,1,0:T(2,128)(2,1)}, u32[]{:S(2)}, u32[]{:S(2)}) async-start(bf16[16,2,512]{2,1,0:T(2,128)(2,1)} %reshape.121), calls=%async_computation.3 | async-start | bytes 65536 | tf_op jit(solution)/shard_map/all_to_all | solution.py:24
  23.4 6.0 %copy-start.6 = (bf16[8,32,2,256]{3,2,1,0:T(2,128)(2,1)}, bf16[8,32,2,256]{3,2,1,0:T(2,128)(2,1)S(1)}, u32[]{:S(2)}) copy-start(bf16[8,32,2,256]{3,2,1,0:T(2,128)(2,1)S(1)} %squeeze.34) | copy-start | bytes 786436
  39.1 2.1 copy-start
  39.1 2.1 copy-start.3
  41.8 1.9 copy-start.2
  59.7 30.3 %all-to-all-start.3 = ((bf16[32,2,256]{2,1,0:T(2,128)(2,1)}), bf16[32,2,256]{2,1,0:T(2,128)(2,1)}, u32[]{:S(2)}, u32[]{:S(2)}) async-start(bf16[32,2,256]{2,1,0:T(2,128)(2,1)} %reshape.123), calls=%async_computation.4 | async-start | bytes 65536 | tf_op jit(solution)/shard_map/all_to_all | solution.py:27
  73.6 115.0 %reduce-scatter.3.cloned.1.call-start = ((), (), s32[]{:S(2)}) async-start(), calls=%async_computation.6 | async-start | bytes 4456448 | tf_op jit(solution)/shard_map/reduce_scatter | solution.py:32
  129.3 2.4 copy-start.13
  131.7 1.3 copy-start.11
  132.9 1.3 copy-start.7
  134.3 2.7 copy-start.16
  134.3 1.4 copy-start.12
  137.0 2.9 copy-start.8
  140.0 1.8 copy-start.1
  140.0 1.8 copy-start.10
  143.5 63.6 %copy-start.15 = (f32[256,32,8]{0,1,2:T(8,128)S(1)}, f32[256,32,8]{0,1,2:T(8,128)}, u32[]{:S(2)}) copy-start(f32[256,32,8]{0,1,2:T(8,128)} %fusion.15) | copy-start | bytes 786436
  191.6 26.6 %all-to-all-start = ((bf16[32,2,256]{2,1,0:T(2,128)(2,1)}), bf16[32,2,256]{2,1,0:T(2,128)(2,1)S(1)}, u32[]{:S(2)}, u32[]{:S(2)}) async-start(bf16[32,2,256]{2,1,0:T(2,128)(2,1)} %reshape.117), calls=%async_computation.1 | async-start | bytes 65536 | tf_op jit(solution)/shard_map/all_to_all | solution.py:33
  204.8 97.6 %reduce-scatter.5.cloned.1.call-start = ((), (), s32[]{:S(2)}) async-start(), calls=%async_computation.7 | async-start | bytes 1114112 | tf_op jit(solution)/shard_map/reduce_scatter | solution.py:43
  222.6 345.8 %all-reduce.3.cloned.1.call-start = ((), (), s32[]{:S(2)}) async-start(), calls=%async_computation.8 | async-start | bytes 1179648 | tf_op jit(solution)/shard_map/psum | solution.py:44
  231.1 2.1 copy-start.9
  236.9 5.0 copy-start.5
Sparse Core Ops, SparseCore 0:
  85.2 103.2 reduce-scatter.2
  222.7 79.6 reduce-scatter.4
  306.0 262.3 all-reduce.2

commit v2 on v1

v2 whole, which is shorter than its diff:
```python
import jax
import jax.numpy as jnp
from jax import lax
from jax.experimental import pallas as pl
from jax.experimental.pallas import tpu as pltpu
from jax.sharding import PartitionSpec as P


BF = jnp.bfloat16
F32 = jnp.float32
MESH = pl.DeviceIdType.MESH
CUTS = 16
IDX = 32

(COT, GEX, RS1, RS2, AG1, AG2, TEX, AMP, ZS2, ZS1, N3, F3, A3, B3, NS, FS, BS, PHASES) = range(18)


def dot(a, b, contract=(1, 0)):
    return lax.dot_general(a, b, (((contract[0],), (contract[1],)), ((), ())), preferred_element_type=F32)


def selection(rows, cols, test):
    r = lax.broadcasted_iota(jnp.int32, (rows, cols), 0)
    c = lax.broadcasted_iota(jnp.int32, (rows, cols), 1)
    return jnp.where(test(r, c), 1.0, 0.0).astype(BF)


def join_lanes(pieces):
    group = lax.broadcasted_iota(jnp.int32, (32, 128), 1) >> 5
    out = None
    for j, (block, off) in enumerate(pieces):
        shift = (32 * j - off) % 128
        moved = pltpu.roll(block, shift, 1) if shift else block
        out = moved if out is None else jnp.where(group == j, moved, out)
    return out


def kernel(b_ref, ws_ref, w3_ref, cot_ref, amp_ref, gs_ref, gl_ref,
           bp, fst, xdc, xnat, w3p, cotr, gcat, grot, gsend, grecv,
           tbuf, trecv, sbuf, recv2, gt, tsend, texr, asend, arecv, bk, b1p,
           z1s, z1r, z2s, z2r, zs3, nr3, fs3, fr3, cls3, zfin,
           ss, nrs, fx, sfin, send_sem, recv_sem):
    cid = lax.axis_index("cuts")
    iid = lax.axis_index("idx")
    core, chip = cid & 1, cid >> 1
    z, xl = iid >> 1, iid & 1
    cls = ((z & 3) << 1) + xl
    far = z >> 2

    def push(phase, src, dst, **device):
        pltpu.make_async_remote_copy(
            src_ref=src, dst_ref=dst, send_sem=send_sem.at[phase], recv_sem=recv_sem.at[phase],
            device_id=device, device_id_type=MESH).start()

    def arrived(phase, ref):
        pltpu.make_async_copy(ref, ref, recv_sem.at[phase]).wait()

    def sent(phase, ref):
        pltpu.make_async_copy(ref, ref, send_sem.at[phase]).wait()

    def others(count, body):
        def step(n, carry):
            body(n)
            return carry
        lax.fori_loop(1, count, step, 0)

    barrier = pltpu.get_barrier_semaphore()
    others(CUTS, lambda n: pl.semaphore_signal(
        barrier, inc=1, device_id={"cuts": (cid + n) & (CUTS - 1)}, device_id_type=MESH))
    others(IDX, lambda n: pl.semaphore_signal(
        barrier, inc=1, device_id={"idx": (iid + n) & (IDX - 1)}, device_id_type=MESH))

    to_dc = selection(256, 256, lambda r, c: ((r >> 5) == (c & 7)) & ((r & 31) == (c >> 3)))
    from_dc = selection(256, 256, lambda r, c: ((c >> 5) == (r & 7)) & ((c & 31) == (r >> 3)))
    row_kc = selection(256, 256, lambda r, c: ((r >> 6) == (c >> 6)) & (((r >> 5) & 1) == (c & 1))
                       & ((r & 31) == ((c >> 1) & 31)))
    w1 = [dot(ws_ref[0, p], from_dc).astype(BF) for p in range(2)]
    for p in range(2):
        for h in range(2):
            rows = slice(256 * h, 256 * h + 256)
            bp[p, rows] = dot(row_kc, b_ref[p, rows]).astype(BF)

    pl.semaphore_wait(barrier, CUTS - 1 + IDX - 1)

    def quarter(c):
        return pl.ds(pl.multiple_of((c >> 2) * 128, 128), 128)

    def send_cot(n):
        to = (cid + n) & (CUTS - 1)
        push(COT, cot_ref.at[:, :, quarter(to)], cotr.at[cid], cuts=to)
    others(CUTS, send_cot)
    cotr[cid] = cot_ref[:, :, quarter(cid)]

    fst[0] = dot(bp[0], w1[0]) - dot(bp[1], w1[1])
    fst[1] = dot(bp[1], w1[0]) + dot(bp[0], w1[1])
    for p in range(2):
        for d in range(8):
            for g in range(4):
                pieces = [(fst[p, 32 * (4 * g + j):32 * (4 * g + j) + 32, 128 * (d // 4):128 * (d // 4) + 128],
                           32 * (d % 4)) for j in range(4)]
                xdc[p, 32 * d:32 * d + 32, 128 * g:128 * g + 128] = join_lanes(pieces).astype(BF)

    arrived(COT, cotr.at[pl.ds(0, CUTS - 1)])
    lane0 = (cid & 3) * 32
    s_re = selection(128, 128, lambda r, c: (c < 32) & (r == c + lane0))
    s_im = selection(128, 128, lambda r, c: (c >= 32) & (c < 64) & (r == c - 32 + lane0))
    g_re = cotr[:, 0].reshape(256, 128)
    g_im = cotr[:, 1].reshape(256, 128)
    gcat[...] = (dot(g_re, s_re) + dot(g_im, s_im)).astype(BF)
    grot[...] = (dot(g_im, s_re) - dot(g_re, s_im)).astype(BF)
    g3b = dot(ws_ref[1, 0], gcat[...]) + dot(ws_ref[1, 1], grot[...])
    gsend[...] = g3b.reshape(IDX, 8, 128)

    def send_g(n):
        to = (iid + n) & (IDX - 1)
        push(GEX, gsend.at[to], grecv.at[iid], idx=to)
    others(IDX, send_g)
    grecv[iid] = gsend[iid]

    for p in range(2):
        w3p[p] = dot(to_dc, w3_ref[p]).astype(BF)
    t_re = dot(w3p[0], xdc[0], (0, 0)) - dot(w3p[1], xdc[1], (0, 0))
    t_im = dot(w3p[0], xdc[1], (0, 0)) + dot(w3p[1], xdc[0], (0, 0))
    for c in range(CUTS):
        tbuf[c & 1, c >> 1, 0] = t_re[16 * c:16 * c + 16].astype(BF)
        tbuf[c & 1, c >> 1, 1] = t_im[16 * c:16 * c + 16].astype(BF)
    push(RS1, tbuf.at[1 - core], trecv, cuts=cid ^ 1)
    for p in range(2):
        xnat[p] = dot(from_dc, xdc[p]).astype(BF)
    arrived(RS1, trecv)
    sbuf[...] = (tbuf[core].astype(F32) + trecv[...].astype(F32)).astype(BF)

    def send_sum(n):
        to = (chip + n) & 7
        push(RS2, sbuf.at[to], recv2.at[chip], cuts=2 * to + core)
    others(8, send_sum)
    recv2[chip] = sbuf[chip]

    arrived(GEX, grecv.at[pl.ds(0, IDX - 1)])
    g_el = grecv[...].reshape(256, 128).astype(BF)
    g_own = None
    for k in range(2):
        pick = selection(128, 128, lambda r, c: (c < 32) & (r < 64) & ((r >> 4) == (c >> 3))
                         & (((r >> 3) & 1) == k) & ((r & 7) == (c & 7)))
        place = selection(256, 512, lambda r, c: ((r & 7) == (c >> 6)) & (((c >> 5) & 1) == k)
                          & ((r >> 3) == (c & 31)))
        part = dot(dot(g_el, pick).astype(BF), place, (0, 0))
        g_own = part if g_own is None else g_own + part
    gt[core, chip] = g_own[:32].astype(BF).reshape(2, 16, 512)

    def send_gather(n):
        to = (chip + n) & 7
        push(AG1, gt.at[core, chip], gt.at[core, chip], cuts=2 * to + core)
    others(8, send_gather)

    arrived(RS2, recv2.at[pl.ds(0, 7)])
    total = recv2[0].astype(F32)
    for g in range(1, 8):
        total = total + recv2[g].astype(F32)
    total = jnp.concatenate([total.reshape(32, 512).astype(BF), jnp.zeros((96, 512), BF)], axis=0)
    to_ekl = selection(512, 512, lambda r, c: ((r >> 4) == (c & 31)) & (((r >> 3) & 1) == ((c >> 5) & 1))
                       & ((r & 7) == (c >> 6)))
    tsend[...] = dot(to_ekl, total, (1, 1)).astype(BF).reshape(IDX, 16, 128)

    def send_t(n):
        to = (iid + n) & (IDX - 1)
        push(TEX, tsend.at[to], texr.at[iid], idx=to)
    others(IDX, send_t)
    texr[iid] = tsend[iid]

    arrived(AG1, gt.at[0, pl.ds(0, 7)])
    push(AG2, gt.at[core], gt.at[core], cuts=cid ^ 1)

    arrived(AG2, gt.at[0])
    gr = jnp.concatenate([gt[c & 1, c >> 1, 0] for c in range(CUTS)], axis=0)
    gi = jnp.concatenate([gt[c & 1, c >> 1, 1] for c in range(CUTS)], axis=0)
    z_re = dot(xnat[0], gr, (1, 1)) + dot(xnat[1], gi, (1, 1))
    z_im = dot(xnat[0], gi, (1, 1)) - dot(xnat[1], gr, (1, 1))
    zs3[0:4] = z_re.astype(BF).reshape(4, 64, 256)
    zs3[4:8] = z_im.astype(BF).reshape(4, 64, 256)

    def near(phase, src, dst):
        for step in (-1, 0, 1, 2):
            for flip in range(2):
                if step or flip:
                    to_z, to_x = (z + step) & 15, xl ^ flip
                    push(phase, src.at[((to_z & 3) << 1) + to_x], dst.at[2 * (step + 1) + flip], idx=2 * to_z + to_x)

    def near_back(phase, src, dst):
        for step in (-1, 0, 1, 2):
            for flip in range(2):
                if step or flip:
                    push(phase, src, dst.at[cls], idx=2 * ((z - step) & 15) + (xl ^ flip))

    near(N3, zs3, nr3)
    nr3[2] = zs3[cls]

    bk[0] = dot(w3p[0], gr) + dot(w3p[1], gi)
    bk[1] = dot(w3p[0], gi) - dot(w3p[1], gr)
    for p in range(2):
        for uk in range(16):
            for g in range(2):
                pieces = [(bk[p, 32 * (4 * g + j):32 * (4 * g + j) + 32, 128 * (uk // 4):128 * (uk // 4) + 128],
                           32 * (uk % 4)) for j in range(4)]
                b1p[p, 32 * uk:32 * uk + 32, 128 * g:128 * g + 128] = join_lanes(pieces).astype(BF)
    z_re = dot(bp[0], b1p[0], (0, 0)) + dot(bp[1], b1p[1], (0, 0))
    z_im = dot(bp[0], b1p[1], (0, 0)) - dot(bp[1], b1p[0], (0, 0))
    z1s[:, 0] = dot(z_re.astype(BF), to_dc).astype(BF).reshape(CUTS, 16, 256)
    z1s[:, 1] = dot(z_im.astype(BF), to_dc).astype(BF).reshape(CUTS, 16, 256)

    def send_cuts(phase, src, dst):
        def one(n):
            to = (cid + n) & (CUTS - 1)
            push(phase, src.at[to], dst.at[cid], cuts=to)
        others(CUTS, one)
        dst[cid] = src[cid]
    send_cuts(ZS1, z1s, z1r)

    arrived(TEX, texr.at[pl.ds(0, IDX - 1)])
    t_all = texr[...].astype(F32).reshape(IDX, 2, 8, 128)
    t_cat = t_rot = None
    for k in range(2):
        t_k = t_all[:, k].reshape(256, 128).astype(BF)
        keep = selection(128, 128, lambda r, c: (r < 32) & (c < 64) & ((r >> 3) == (c >> 4))
                         & (((c >> 3) & 1) == k) & ((r & 7) == (c & 7)))
        from_im = selection(128, 128, lambda r, c: (r >= 16) & (r < 32) & (c < 32) & (((r - 16) >> 3) == (c >> 4))
                            & (((c >> 3) & 1) == k) & ((r & 7) == (c & 7)))
        from_re = selection(128, 128, lambda r, c: (r < 16) & (c >= 32) & (c < 64) & ((r >> 3) == ((c - 32) >> 4))
                            & (((c >> 3) & 1) == k) & ((r & 7) == (c & 7)))
        one, two = dot(t_k, keep), dot(t_k, from_re) - dot(t_k, from_im)
        t_cat = one if t_cat is None else t_cat + one
        t_rot = two if t_rot is None else t_rot + two
    t_cat, t_rot = t_cat.astype(BF), t_rot.astype(BF)
    amp = dot(ws_ref[1, 0], t_cat, (0, 0)) + dot(ws_ref[1, 1], t_rot, (0, 0))
    asend[...] = amp.reshape(CUTS, 16, 128)
    send_cuts(AMP, asend, arecv)
    z2s[:, 0] = dot(t_cat, gcat[...], (1, 1)).astype(BF).reshape(CUTS, 16, 256)
    z2s[:, 1] = dot(t_cat, grot[...], (1, 1)).astype(BF).reshape(CUTS, 16, 256)
    send_cuts(ZS2, z2s, z2r)

    def add_up(ref, count):
        out = ref[0].astype(F32)
        for n in range(1, count):
            out = out + ref[n].astype(F32)
        return out

    arrived(N3, nr3.at[pl.ds(0, 7)])
    fs3[...] = add_up(nr3, 8).astype(BF).reshape(4, 16, 256)
    for hop in range(1, 4):
        to_far = (far + hop) & 3
        push(F3, fs3.at[to_far], fr3.at[far], idx=2 * (4 * to_far + (z & 3)) + xl)
    fr3[far] = fs3[far]

    arrived(ZS1, z1r.at[pl.ds(0, CUTS - 1)])
    ss[0:4] = add_up(z1r, CUTS).reshape(4, 8, 256)
    arrived(ZS2, z2r.at[pl.ds(0, CUTS - 1)])
    ss[4:8] = add_up(z2r, CUTS).reshape(4, 8, 256)
    near(NS, ss, nrs)
    nrs[2] = ss[cls]

    arrived(F3, fr3.at[pl.ds(0, 3)])
    cls3[far] = add_up(fr3, 4).astype(BF)
    for hop in range(1, 4):
        push(A3, cls3.at[far], cls3.at[far], idx=2 * (4 * ((far + hop) & 3) + (z & 3)) + xl)

    arrived(NS, nrs.at[pl.ds(0, 7)])
    fx[far] = add_up(nrs, 8)
    for hop in range(1, 4):
        push(FS, fx.at[far], fx.at[far], idx=2 * (4 * ((far + hop) & 3) + (z & 3)) + xl)

    arrived(A3, cls3.at[pl.ds(0, 3)])
    near_back(B3, cls3, zfin)
    zfin[cls] = cls3[...]

    arrived(FS, fx.at[pl.ds(0, 3)])
    sfin[cls] = add_up(fx, 4)
    near_back(BS, sfin.at[cls], sfin)

    arrived(AMP, arecv.at[pl.ds(0, CUTS - 1)])
    for p in range(2):
        for g in range(4):
            for h in range(2):
                rows = slice(8 * h, 8 * h + 8)
                group = lax.broadcasted_iota(jnp.int32, (8, 128), 1) >> 5
                out = None
                for j in range(4):
                    block = arecv[4 * g + j, rows]
                    shift = (32 * j - 32 * p) % 128
                    moved = pltpu.roll(block, shift, 1) if shift else block
                    out = moved if out is None else jnp.where(group == j, moved, out)
                amp_ref[p, rows, 128 * g:128 * g + 128] = out
    arrived(B3, zfin.at[pl.ds(0, 7)])
    for n in range(8):
        gl_ref[n // 4, 64 * (n % 4):64 * (n % 4) + 64] = zfin[n].reshape(64, 256).astype(F32)
    arrived(BS, sfin.at[pl.ds(0, 7)])
    gs_ref[...] = sfin[...].reshape(64, 256)

    sent(COT, cotr.at[pl.ds(0, CUTS - 1)])
    sent(GEX, grecv.at[pl.ds(0, IDX - 1)])
    sent(RS1, trecv)
    sent(RS2, recv2.at[pl.ds(0, 7)])
    sent(AG1, gt.at[0, pl.ds(0, 7)])
    sent(AG2, gt.at[0])
    sent(TEX, texr.at[pl.ds(0, IDX - 1)])
    sent(AMP, arecv.at[pl.ds(0, CUTS - 1)])
    sent(ZS2, z2r.at[pl.ds(0, CUTS - 1)])
    sent(ZS1, z1r.at[pl.ds(0, CUTS - 1)])
    sent(N3, nr3.at[pl.ds(0, 7)])
    sent(F3, fr3.at[pl.ds(0, 3)])
    sent(A3, cls3.at[pl.ds(0, 3)])
    sent(B3, zfin.at[pl.ds(0, 7)])
    sent(NS, nrs.at[pl.ds(0, 7)])
    sent(FS, fx.at[pl.ds(0, 3)])
    sent(BS, sfin.at[pl.ds(0, 7)])


def local(boundary, gates_shared, gates_sliced, cotangent):
    vmem = pltpu.VMEM
    scratch = [
        vmem((2, 512, 256), BF),
        vmem((2, 512, 256), F32),
        vmem((2, 256, 512), BF),
        vmem((2, 256, 512), BF),
        vmem((2, 256, 256), BF),
        vmem((CUTS, 2, 16, 128), BF),
        vmem((256, 128), BF),
        vmem((256, 128), BF),
        vmem((IDX, 8, 128), F32),
        vmem((IDX, 8, 128), F32),
        vmem((2, 8, 2, 16, 512), BF),
        vmem((8, 2, 16, 512), BF),
        vmem((8, 2, 16, 512), BF),
        vmem((8, 2, 16, 512), BF),
        vmem((2, 8, 2, 16, 512), BF),
        vmem((IDX, 16, 128), BF),
        vmem((IDX, 16, 128), BF),
        vmem((CUTS, 16, 128), F32),
        vmem((CUTS, 16, 128), F32),
        vmem((2, 256, 512), F32),
        vmem((2, 512, 256), BF),
        vmem((CUTS, 2, 16, 256), BF),
        vmem((CUTS, 2, 16, 256), BF),
        vmem((CUTS, 2, 16, 256), BF),
        vmem((CUTS, 2, 16, 256), BF),
        vmem((8, 64, 256), BF),
        vmem((8, 64, 256), BF),
        vmem((4, 16, 256), BF),
        vmem((4, 16, 256), BF),
        vmem((4, 16, 256), BF),
        vmem((8, 4, 16, 256), BF),
        vmem((8, 8, 256), F32),
        vmem((8, 8, 256), F32),
        vmem((4, 8, 256), F32),
        vmem((8, 8, 256), F32),
        pltpu.SemaphoreType.DMA((PHASES,)),
        pltpu.SemaphoreType.DMA((PHASES,)),
    ]
    amp, shared, sliced = pl.pallas_call(
        kernel,
        out_shape=(
            jax.ShapeDtypeStruct((2, 16, 512), F32),
            jax.ShapeDtypeStruct((64, 256), F32),
            jax.ShapeDtypeStruct((2, 256, 256), F32),
        ),
        in_specs=[pl.BlockSpec(memory_space=vmem)] * 4,
        out_specs=[pl.BlockSpec(memory_space=vmem)] * 3,
        scratch_shapes=scratch,
        compiler_params=pltpu.CompilerParams(
            collective_id=0, has_side_effects=True, vmem_limit_bytes=40 * 2 ** 20),
    )(boundary.reshape(2, 512, 256), gates_shared, gates_sliced[:, 0], cotangent[:, 0])
    return amp[:, None], shared.reshape(2, 2, 16, 256), sliced[:, None]


def solution(mesh):
    return jax.shard_map(
        local,
        mesh=mesh,
        in_specs=(
            P(None, "cuts", "idx"),
            P(),
            P(None, "cuts", None, None),
            P(None, "idx", "cuts", None),
        ),
        out_specs=(
            P(None, "idx", "cuts", None),
            P(None, None, "cuts", None),
            P(None, "cuts", None, None),
        ),
        check_vma=False,
    )
```

time: 580 us -> 74.7 us (0.13)
  the two profiles are of different devices: /device:TPU:4 before, /device:TPU:2 now
where the time goes in v2:
time: 74.7 us; the launch traced here: 74.6 us
  Pallas kernels  70.6 us (95%)
  local copies, waits for them, and re-layouts  3.29 us (4%)
    pallas_call x1, Pallas kernels, local(): pl.pallas_call(kernel, out_shape=(jax.ShapeDtypeStruct((2, 16, 512), F32)...  70.6 us
    unnamed x10, local copies, waits for them, and re-layouts  3.29 us

profile of v2, /device:TPU:2, one launch (start us, length us, event | category | flops | bytes accessed | tf_op | source)
XLA Modules:
  0.0 74.6 jit_solution(13815140081475121761)
XLA Ops:
  0.6 0.0 copy-start
  0.6 0.0 copy-start.1
  0.7 0.0 copy-start.2
  0.7 1.2 %copy.11 = bf16[1,2,512,256]{3,2,1,0:T(8,128)(2,1)S(1)} copy(bf16[1,2,512,256]{3,1,2,0:T(2,128)(2,1)} %bitcast.21) | data formatting | bytes 1048576
  1.8 0.0 copy-done
  1.9 0.0 copy-done.1
  1.9 0.0 copy-done.2
  1.9 70.6 %shard_map.67 = (f32[2,16,512]{2,1,0:T(8,128)S(1)}, f32[64,256]{1,0:T(8,128)S(1)}, f32[2,256,256]{2,1,0:T(8,128)S(1)}) custom-call(bf16[2,512,256]{2,1,0:T(8,128)(2,1)S(1)} %bitcast.15, bf16[2,2,256,256]{3,2,1,0:T(8,128)(2,1)S(1)} %copy-done, bf16[2,256,256]{2,1,0:T(8,128)(2,1)S(1)} %bitcast.17, bf16[2,16,512]{2,1,0:T(8,128)(2,1)S(1)} %bitcast.20), custom_call_target="tpu_custom_call" | custom-call | tf_op jit(solution)/shard_map/pallas_call | solution.py:358
  72.5 0.6 copy.15
  73.2 0.6 copy.16
  73.8 0.8 %copy.17 = f32[2,1,256,256]{3,2,1,0:T(8,128)} copy(f32[2,1,256,256]{3,2,1,0:T(8,128)S(1)} %bitcast.16) | data formatting | bytes 1048576
Async XLA Ops:
  0.6 1.2 %copy-start = (bf16[2,2,256,256]{3,2,1,0:T(8,128)(2,1)S(1)}, bf16[2,2,256,256]{3,2,1,0:T(8,128)(2,1)}, u32[]{:S(2)}) copy-start(bf16[2,2,256,256]{3,2,1,0:T(8,128)(2,1)} %ws_ref.1) | copy-start | bytes 1572868
  0.6 1.3 %copy-start.1 = (bf16[2,1,256,256]{3,2,1,0:T(8,128)(2,1)S(1)}, bf16[2,1,256,256]{3,2,1,0:T(8,128)(2,1)}, u32[]{:S(2)}) copy-start(bf16[2,1,256,256]{3,2,1,0:T(8,128)(2,1)} %param.6) | copy-start | bytes 786436
  0.7 1.2 %copy-start.2 = (bf16[2,1,16,512]{3,2,1,0:T(8,128)(2,1)S(1)}, bf16[2,1,16,512]{3,2,1,0:T(8,128)(2,1)}, u32[]{:S(2)}) copy-start(bf16[2,1,16,512]{3,2,1,0:T(8,128)(2,1)} %param.7) | copy-start | bytes 98308

commit v3 on v1

v3 whole, which is shorter than its diff:
```python
import jax
import jax.numpy as jnp
from jax import lax
from jax.experimental import pallas as pl
from jax.experimental.pallas import tpu as pltpu
from jax.sharding import PartitionSpec as P


BF = jnp.bfloat16
F32 = jnp.float32
MESH = pl.DeviceIdType.MESH
CUTS = 16

(COT, GEX, RS1, RS2, AG1, AG2, TEX, AMP, ZS2, ZS1, N3A, N3B, F3, B3, NS, FS, BS, PHASES) = range(18)

LINE = sorted(range(1, 16), key=lambda n: -min(n, 16 - n))
NEAR = [(2, 1), (2, 0), (-1, 1), (1, 1), (-1, 0), (1, 0), (0, 1)]


def hops(dy, dx, dc, flip):
    return min(dy, 4 - dy) + (2 if dx > flip else max(dx, flip)) + 0.5 * dc


CUT_STEPS = sorted(((dy, dx, dc) for dy in range(4) for dx in range(2) for dc in range(2) if dy + dx + dc),
                   key=lambda t: -hops(*t, 0))
PLANE_STEPS = sorted(((dy, dx, flip) for dy in range(4) for dx in range(2) for flip in range(2) if dy + dx + flip),
                     key=lambda t: -hops(t[0], t[1], 0, t[2]))


def dot(a, b, contract=(1, 0)):
    return lax.dot_general(a, b, (((contract[0],), (contract[1],)), ((), ())), preferred_element_type=F32)


def selection(rows, cols, test):
    r = lax.broadcasted_iota(jnp.int32, (rows, cols), 0)
    c = lax.broadcasted_iota(jnp.int32, (rows, cols), 1)
    return jnp.where(test(r, c), 1.0, 0.0).astype(BF)


def join_lanes(pieces):
    group = lax.broadcasted_iota(jnp.int32, (32, 128), 1) >> 5
    out = None
    for j, (block, off) in enumerate(pieces):
        shift = (32 * j - off) % 128
        moved = pltpu.roll(block, shift, 1) if shift else block
        out = moved if out is None else jnp.where(group == j, moved, out)
    return out


def kernel(b_ref, ws_ref, w3_ref, cot_ref, amp_ref, gs_ref, gl_ref,
           bp, fst, xdc, xp, xnat, w3p, cotr, gcat, grot, gsend, grecv, gown,
           tbuf, trecv, sbuf, recv2, gt, tsend, texr, asend, arecv, bk, b1p,
           z1s, z1r, z2s, z2r, zs3, nr3, clsx, cls3, zfin,
           ss, nrs, fx, sfin, send_sem, recv_sem):
    cid = lax.axis_index("cuts")
    iid = lax.axis_index("idx")
    y, xh, core, chip = cid >> 2, (cid >> 1) & 1, cid & 1, cid >> 1
    z, xl = iid >> 1, iid & 1
    cls = ((z & 3) << 1) + xl
    far = z >> 2

    totals = {
        COT: cotr.at[pl.ds(0, 15)], GEX: grecv.at[pl.ds(0, 15)], RS1: trecv, RS2: recv2.at[pl.ds(0, 15)],
        AG1: gt.at[0, pl.ds(0, 15)], AG2: gt.at[0], TEX: texr.at[pl.ds(0, 15)], AMP: arecv.at[pl.ds(0, 15)],
        ZS2: z2r.at[pl.ds(0, 15)], ZS1: z1r.at[pl.ds(0, 15)], N3A: nr3.at[0, pl.ds(0, 7)],
        N3B: nr3.at[0, pl.ds(0, 7)], F3: clsx.at[pl.ds(0, 3)], B3: zfin.at[pl.ds(0, 7)],
        NS: nrs.at[pl.ds(0, 7)], FS: fx.at[pl.ds(0, 3)], BS: sfin.at[pl.ds(0, 7)]}
    started = []

    def push(phase, src, dst, cuts=None, idx=None):
        if phase not in started:
            started.append(phase)
        device = {}
        if cuts is not None:
            device["cuts"] = cuts
        if idx is not None:
            device["idx"] = idx
        pltpu.make_async_remote_copy(
            src_ref=src, dst_ref=dst, send_sem=send_sem.at[phase], recv_sem=recv_sem.at[phase],
            device_id=device, device_id_type=MESH).start()

    def arrived(phase):
        pltpu.make_async_copy(totals[phase], totals[phase], recv_sem.at[phase]).wait()

    def chip_at(dy, dx):
        return (((y + dy) & 3) << 1) + (xh ^ dx)

    barrier = pltpu.get_barrier_semaphore()

    def greet(**device):
        pl.semaphore_signal(barrier, inc=1, device_id=device, device_id_type=MESH)
    for n in LINE:
        greet(idx=2 * ((z + n) & 15) + xl)
    for n in (2, 14, 1, 15):
        greet(idx=2 * ((z + n) & 15) + (xl ^ 1))
    for dy, dx, dc in CUT_STEPS:
        greet(cuts=2 * chip_at(dy, dx) + (core ^ dc))
    for dy in range(4):
        for dx in range(2):
            greet(cuts=2 * chip_at(dy, dx) + core, idx=iid ^ 1)

    to_dc = selection(256, 256, lambda r, c: ((r >> 5) == (c & 7)) & ((r & 31) == (c >> 3)))
    from_dc = selection(256, 256, lambda r, c: ((c >> 5) == (r & 7)) & ((c & 31) == (r >> 3)))
    row_kc = selection(256, 256, lambda r, c: ((r >> 6) == (c >> 6)) & (((r >> 5) & 1) == (c & 1))
                       & ((r & 31) == ((c >> 1) & 31)))
    to_xlkz = selection(512, 512, lambda r, c: ((r & 1) == (c >> 8)) & (((r >> 1) & 15) == (c & 15))
                        & (((r >> 5) & 1) == ((c >> 4) & 1)) & ((r >> 6) == ((c >> 5) & 7)))

    pl.semaphore_wait(barrier, 42)

    def quarter(c):
        return pl.ds(pl.multiple_of((c >> 2) * 128, 128), 128)

    for dy, dx, dc in CUT_STEPS:
        to = 2 * chip_at(dy, dx) + (core ^ dc)
        push(COT, cot_ref.at[:, :, quarter(to)], cotr.at[cid], cuts=to)
    cotr[cid] = cot_ref[:, :, quarter(cid)]

    w1 = [dot(ws_ref[0, p], from_dc).astype(BF) for p in range(2)]
    for p in range(2):
        for h in range(2):
            rows = slice(256 * h, 256 * h + 256)
            bp[p, rows] = dot(row_kc, b_ref[p, rows]).astype(BF)
    fst[0] = dot(bp[0], w1[0]) - dot(bp[1], w1[1])
    fst[1] = dot(bp[1], w1[0]) + dot(bp[0], w1[1])
    for p in range(2):
        for d in range(8):
            for g in range(4):
                pieces = [(fst[p, 32 * (4 * g + j):32 * (4 * g + j) + 32, 128 * (d // 4):128 * (d // 4) + 128],
                           32 * (d % 4)) for j in range(4)]
                xdc[p, 32 * d:32 * d + 32, 128 * g:128 * g + 128] = join_lanes(pieces).astype(BF)
        xp[p] = dot(xdc[p], to_xlkz).astype(BF)

    for p in range(2):
        w3p[p] = dot(to_dc, w3_ref[p]).astype(BF)
    t_re = dot(w3p[0], xp[0], (0, 0)) - dot(w3p[1], xp[1], (0, 0))
    t_im = dot(w3p[0], xp[1], (0, 0)) + dot(w3p[1], xp[0], (0, 0))
    for c in range(CUTS):
        for x in range(2):
            rows, lanes = slice(16 * c, 16 * c + 16), slice(256 * x, 256 * x + 256)
            tbuf[c & 1, 8 * x + (c >> 1), 0] = t_re[rows, lanes].astype(BF)
            tbuf[c & 1, 8 * x + (c >> 1), 1] = t_im[rows, lanes].astype(BF)
    push(RS1, tbuf.at[1 - core], trecv, cuts=cid ^ 1)
    for p in range(2):
        xnat[p] = dot(from_dc, xp[p]).astype(BF)
    arrived(RS1)
    sbuf[...] = (tbuf[core].astype(F32) + trecv[...].astype(F32)).astype(BF)
    for dy, dx, flip in PLANE_STEPS:
        to, to_x = chip_at(dy, dx), xl ^ flip
        push(RS2, sbuf.at[8 * to_x + to], recv2.at[8 * xl + chip], cuts=2 * to + core, idx=2 * z + to_x)
    recv2[8 * xl + chip] = sbuf[8 * xl + chip]

    arrived(COT)
    lane0 = (cid & 3) * 32
    s_re = selection(128, 128, lambda r, c: (c < 32) & (r == c + lane0))
    s_im = selection(128, 128, lambda r, c: (c >= 32) & (c < 64) & (r == c - 32 + lane0))
    g_re = cotr[:, 0].reshape(256, 128)
    g_im = cotr[:, 1].reshape(256, 128)
    gcat[...] = (dot(g_re, s_re) + dot(g_im, s_im)).astype(BF)
    grot[...] = (dot(g_im, s_re) - dot(g_re, s_im)).astype(BF)
    g3b = dot(ws_ref[1, 0], gcat[...]) + dot(ws_ref[1, 1], grot[...])
    gsend[...] = g3b.astype(BF).reshape(16, 16, 128)
    for n in LINE:
        to = (z + n) & 15
        push(GEX, gsend.at[to], grecv.at[z], idx=2 * to + xl)
    grecv[z] = gsend[z]

    arrived(RS2)
    rows = []
    for x in range(2):
        part = recv2[8 * x].astype(F32)
        for g in range(1, 8):
            part = part + recv2[8 * x + g].astype(F32)
        rows.append(part.reshape(32, 256).astype(BF))
    rows.append(jnp.zeros((64, 256), BF))
    to_zkl = selection(256, 256, lambda r, c: ((r >> 4) == (c & 15)) & (((r >> 3) & 1) == ((c >> 4) & 1))
                       & ((r & 7) == (c >> 5)))
    tsend[...] = dot(to_zkl, jnp.concatenate(rows, axis=0), (1, 1)).astype(BF).reshape(16, 16, 128)
    for n in LINE:
        to = (z + n) & 15
        push(TEX, tsend.at[to], texr.at[z], idx=2 * to + xl)
    texr[z] = tsend[z]

    arrived(GEX)
    g_all = grecv[...].astype(F32).reshape(16, 2, 8, 128)
    for x in range(2):
        g_zl = g_all[:, x].reshape(128, 128).astype(BF)
        out = None
        for k in range(2):
            pick = selection(128, 128, lambda r, c: (c < 32) & (r < 64) & ((r >> 4) == (c >> 3))
                             & (((r >> 3) & 1) == k) & ((r & 7) == (c & 7)))
            place = selection(128, 256, lambda r, c: ((r & 7) == (c >> 5)) & (((c >> 4) & 1) == k)
                              & ((r >> 3) == (c & 15)))
            part = dot(dot(g_zl, pick).astype(BF), place, (0, 0))
            out = part if out is None else out + part
        gown[x] = out[:32].astype(BF).reshape(2, 16, 256)
    for dy, dx, flip in PLANE_STEPS:
        to_x = xl ^ flip
        push(AG1, gown.at[to_x], gt.at[core, 2 * chip + xl], cuts=2 * chip_at(dy, dx) + core, idx=2 * z + to_x)
    gt[core, 2 * chip + xl] = gown[xl]

    def push_cuts(phase, src, dst):
        for dy, dx, dc in CUT_STEPS:
            to = 2 * chip_at(dy, dx) + (core ^ dc)
            push(phase, src.at[to], dst.at[cid], cuts=to)
        dst[cid] = src[cid]

    arrived(TEX)
    t_all = texr[...].astype(F32).reshape(16, 2, 8, 128)
    t_k = [t_all[:, k].reshape(128, 128).astype(BF) for k in range(2)]
    cat, rot = [], []
    for x in range(2):
        one = two = None
        for k in range(2):
            def same(r, c):
                return (c < 64) & ((r >> 5) == x) & (((c >> 3) & 1) == k) & ((r & 7) == (c & 7)) \
                    & (((r >> 3) & 1) == ((c >> 4) & 1))
            keep = selection(128, 128, lambda r, c: same(r, c) & (((r >> 4) & 1) == (c >> 5)))
            to_im = selection(128, 128, lambda r, c: same(r, c) & (((r >> 4) & 1) == 0) & (c >= 32))
            to_re = selection(128, 128, lambda r, c: same(r, c) & (((r >> 4) & 1) == 1) & (c < 32))
            a, b = dot(t_k[k], keep), dot(t_k[k], to_im - to_re)
            one, two = (a, b) if one is None else (one + a, two + b)
        cat.append(one.astype(BF))
        rot.append(two.astype(BF))
    to_u = selection(256, 256, lambda r, c: ((r >> 4) == ((c >> 3) & 15)) & (((r >> 3) & 1) == (c >> 7))
                     & ((r & 7) == (c & 7)))
    t_cat = dot(to_u, jnp.concatenate(cat, axis=0)).astype(BF)
    t_rot = dot(to_u, jnp.concatenate(rot, axis=0)).astype(BF)
    amp = dot(ws_ref[1, 0], t_cat, (0, 0)) + dot(ws_ref[1, 1], t_rot, (0, 0))
    asend[...] = amp.reshape(CUTS, 16, 128)
    z2s[:, 0] = dot(t_cat, gcat[...], (1, 1)).astype(BF).reshape(CUTS, 16, 256)
    z2s[:, 1] = dot(t_cat, grot[...], (1, 1)).astype(BF).reshape(CUTS, 16, 256)
    push_cuts(ZS2, z2s, z2r)
    push_cuts(AMP, asend, arecv)

    def near(phase, src, dst):
        for step, flip in NEAR:
            to_z, to_x = (z + step) & 15, xl ^ flip
            push(phase, src.at[((to_z & 3) << 1) + to_x], dst.at[2 * (step + 1) + flip], idx=2 * to_z + to_x)
        dst[2] = src[cls]

    def near_back(phase, src, dst):
        for step, flip in NEAR:
            push(phase, src, dst.at[cls], idx=2 * ((z - step) & 15) + (xl ^ flip))

    def grad_three(half, phase):
        g = [jnp.concatenate([jnp.concatenate([gt[half, 2 * n, p], gt[half, 2 * n + 1, p]], axis=1)
                              for n in range(8)], axis=0) for p in range(2)]
        z_re = dot(xnat[0], g[0], (1, 1)) + dot(xnat[1], g[1], (1, 1))
        z_im = dot(xnat[0], g[1], (1, 1)) - dot(xnat[1], g[0], (1, 1))
        zs3[half, 0:4] = z_re.astype(BF).reshape(4, 64, 128)
        zs3[half, 4:8] = z_im.astype(BF).reshape(4, 64, 128)
        near(phase, zs3.at[half], nr3.at[half])

    arrived(AG1)
    push(AG2, gt.at[core], gt.at[core], cuts=cid ^ 1)
    grad_three(core, N3A)
    arrived(AG2)
    grad_three(1 - core, N3B)

    gr, gi = [
        dot(jnp.concatenate([jnp.concatenate([gt[c & 1, 2 * (c >> 1), p], gt[c & 1, 2 * (c >> 1) + 1, p]], axis=1)
                             for c in range(CUTS)], axis=0), to_xlkz, (1, 1)).astype(BF) for p in range(2)]
    bk[0] = dot(w3p[0], gr) + dot(w3p[1], gi)
    bk[1] = dot(w3p[0], gi) - dot(w3p[1], gr)
    for p in range(2):
        for uk in range(16):
            for g in range(2):
                pieces = [(bk[p, 32 * (4 * g + j):32 * (4 * g + j) + 32, 128 * (uk // 4):128 * (uk // 4) + 128],
                           32 * (uk % 4)) for j in range(4)]
                b1p[p, 32 * uk:32 * uk + 32, 128 * g:128 * g + 128] = join_lanes(pieces).astype(BF)
    z_re = dot(bp[0], b1p[0], (0, 0)) + dot(bp[1], b1p[1], (0, 0))
    z_im = dot(bp[0], b1p[1], (0, 0)) - dot(bp[1], b1p[0], (0, 0))
    z1s[:, 0] = dot(z_re.astype(BF), to_dc).astype(BF).reshape(CUTS, 16, 256)
    z1s[:, 1] = dot(z_im.astype(BF), to_dc).astype(BF).reshape(CUTS, 16, 256)
    push_cuts(ZS1, z1s, z1r)

    def add_up(ref, count):
        out = ref[0].astype(F32)
        for n in range(1, count):
            out = out + ref[n].astype(F32)
        return out

    def push_far(phase, ref):
        for hop in (2, 1, 3):
            push(phase, ref.at[far], ref.at[far], idx=2 * (4 * ((far + hop) & 3) + (z & 3)) + xl)

    arrived(N3A)
    arrived(N3B)
    for half in range(2):
        clsx[far, half] = add_up(nr3.at[half], 8).astype(BF)
    push_far(F3, clsx)

    arrived(ZS2)
    ss[4:8] = add_up(z2r, CUTS).reshape(4, 8, 256)
    arrived(ZS1)
    ss[0:4] = add_up(z1r, CUTS).reshape(4, 8, 256)
    near(NS, ss, nrs)

    arrived(F3)
    cls3[...] = add_up(clsx, 4).astype(BF)
    near_back(B3, cls3, zfin)
    zfin[cls] = cls3[...]

    arrived(NS)
    fx[far] = add_up(nrs, 8)
    push_far(FS, fx)

    arrived(AMP)
    group = lax.broadcasted_iota(jnp.int32, (8, 128), 1) >> 5
    for p in range(2):
        for g in range(4):
            for h in range(2):
                rows = slice(8 * h, 8 * h + 8)
                out = None
                for j in range(4):
                    block = arecv[4 * g + j, rows]
                    shift = (32 * j - 32 * p) % 128
                    moved = pltpu.roll(block, shift, 1) if shift else block
                    out = moved if out is None else jnp.where(group == j, moved, out)
                amp_ref[p, rows, 128 * g:128 * g + 128] = out

    arrived(FS)
    sfin[cls] = add_up(fx, 4)
    near_back(BS, sfin.at[cls], sfin)

    to_cut = selection(256, 256, lambda r, c: ((r >> 7) == ((c >> 4) & 1)) & (((r >> 4) & 7) == (c >> 5))
                       & ((r & 15) == (c & 15)))
    arrived(B3)
    for n in range(8):
        block = jnp.concatenate([zfin[n, 0], zfin[n, 1]], axis=1)
        gl_ref[n // 4, 64 * (n % 4):64 * (n % 4) + 64] = dot(block, to_cut)
    arrived(BS)
    gs_ref[...] = sfin[...].reshape(64, 256)

    for phase in started:
        pltpu.make_async_copy(totals[phase], totals[phase], send_sem.at[phase]).wait()


def local(boundary, gates_shared, gates_sliced, cotangent):
    vmem = pltpu.VMEM
    scratch = [
        vmem((2, 512, 256), BF),
        vmem((2, 512, 256), F32),
        vmem((2, 256, 512), BF),
        vmem((2, 256, 512), BF),
        vmem((2, 256, 512), BF),
        vmem((2, 256, 256), BF),
        vmem((CUTS, 2, 16, 128), BF),
        vmem((256, 128), BF),
        vmem((256, 128), BF),
        vmem((16, 16, 128), BF),
        vmem((16, 16, 128), BF),
        vmem((2, 2, 16, 256), BF),
        vmem((2, 16, 2, 16, 256), BF),
        vmem((16, 2, 16, 256), BF),
        vmem((16, 2, 16, 256), BF),
        vmem((16, 2, 16, 256), BF),
        vmem((2, 16, 2, 16, 256), BF),
        vmem((16, 16, 128), BF),
        vmem((16, 16, 128), BF),
        vmem((CUTS, 16, 128), F32),
        vmem((CUTS, 16, 128), F32),
        vmem((2, 256, 512), F32),
        vmem((2, 512, 256), BF),
        vmem((CUTS, 2, 16, 256), BF),
        vmem((CUTS, 2, 16, 256), BF),
        vmem((CUTS, 2, 16, 256), BF),
        vmem((CUTS, 2, 16, 256), BF),
        vmem((2, 8, 64, 128), BF),
        vmem((2, 8, 64, 128), BF),
        vmem((4, 2, 64, 128), BF),
        vmem((2, 64, 128), BF),
        vmem((8, 2, 64, 128), BF),
        vmem((8, 8, 256), F32),
        vmem((8, 8, 256), F32),
        vmem((4, 8, 256), F32),
        vmem((8, 8, 256), F32),
        pltpu.SemaphoreType.DMA((PHASES,)),
        pltpu.SemaphoreType.DMA((PHASES,)),
    ]
    amp, shared, sliced = pl.pallas_call(
        kernel,
        out_shape=(
            jax.ShapeDtypeStruct((2, 16, 512), F32),
            jax.ShapeDtypeStruct((64, 256), F32),
            jax.ShapeDtypeStruct((2, 256, 256), F32),
        ),
        in_specs=[pl.BlockSpec(memory_space=vmem)] * 4,
        out_specs=[pl.BlockSpec(memory_space=vmem)] * 3,
        scratch_shapes=scratch,
        compiler_params=pltpu.CompilerParams(
            collective_id=0, has_side_effects=True, vmem_limit_bytes=40 * 2 ** 20),
    )(boundary.reshape(2, 512, 256), gates_shared, gates_sliced[:, 0], cotangent[:, 0])
    return amp[:, None], shared.reshape(2, 2, 16, 256), sliced[:, None]


def solution(mesh):
    return jax.shard_map(
        local,
        mesh=mesh,
        in_specs=(
            P(None, "cuts", "idx"),
            P(),
            P(None, "cuts", None, None),
            P(None, "idx", "cuts", None),
        ),
        out_specs=(
            P(None, "idx", "cuts", None),
            P(None, None, "cuts", None),
            P(None, "cuts", None, None),
        ),
        check_vma=False,
    )
```

time: 580 us -> 69 us (0.12)
  waiting for transfers between devices: 367 us -> 0 us
  local copies, waits for them, and re-layouts: 70.1 us -> 3.29 us
  Pallas kernels: 0 us -> 64.9 us
  blocking collectives: 42 us -> 0 us
  starting transfers between devices: 37.3 us -> 0 us
  matrix products: 33.9 us -> 0 us
  between operations: 14.3 us -> 0.68 us
  other arithmetic: 13.2 us -> 0 us
    psum x1 -> x0, waiting for transfers between devices: 252 us -> none  [local(): shared, sliced = lax.psum((shared, grad_three), 'idx')]
    reduce_scatter x2 -> x0, waiting for transfers between devices: 105 us -> none  [the longest x1 60.4 us: local(): shared = lax.psum_scatter(shared, 'cuts', scatter_dimension=2, tiled=True)]
    pallas_call x0 -> x1, Pallas kernels: none -> 64.9 us  [local(): pl.pallas_call(kernel, out_shape=(jax.ShapeDtypeStruct((2, 16, 512), F32)...]
    all_to_all x3 -> x0, starting transfers between devices: 36.9 us -> none  [the longest x1 13.9 us: local(): g3b = lax.all_to_all(g3b, 'idx', split_axis=1, concat_axis=1, tiled=True)]
    dot_general x32 -> x0, matrix products: 33.9 us -> none  [one(): jnp.einsum(formula, left[a], right[b], preferred_element_type=jnp.float32)]
    all_gather x1 -> x0, blocking collectives: 31.6 us -> none  [local(): g3b = lax.all_gather(g3b, 'cuts', axis=3, tiled=True)]
    squeeze x12 -> x0, local copies, waits for them, and re-layouts: 23.1 us -> none  [the longest x6 16.6 us: one(): right[b]]
    another operation x8 -> x0, local copies, waits for them, and re-layouts: 17.2 us -> none  [the longest x6 15.7 us: cdot(): return jnp.stack([real, imag])]
  transfers between devices with their start and end apart: 6 -> 0, of which waited for: 4 -> 0; matrix products, arithmetic and copies ran while one was open for 16% -> 0% of each run, Pallas kernels for 0% -> 0%
where the time goes in v3:
time: 69 us; the launch traced here: 68.9 us
  Pallas kernels  64.9 us (94%)
  local copies, waits for them, and re-layouts  3.29 us (5%)
    pallas_call x1, Pallas kernels, local(): pl.pallas_call(kernel, out_shape=(jax.ShapeDtypeStruct((2, 16, 512), F32)...  64.9 us
    unnamed x10, local copies, waits for them, and re-layouts  3.29 us

profile of v3, /device:TPU:4, one launch (start us, length us, event | category | flops | bytes accessed | tf_op | source)
XLA Modules:
  0.0 68.9 jit_solution(1549417019590859547)
XLA Ops:
  0.6 0.0 copy-start
  0.6 0.0 copy-start.1
  0.7 0.0 copy-start.2
  0.7 1.2 %copy.11 = bf16[1,2,512,256]{3,2,1,0:T(8,128)(2,1)S(1)} copy(bf16[1,2,512,256]{3,1,2,0:T(2,128)(2,1)} %bitcast.21) | data formatting | bytes 1048576
  1.8 0.0 copy-done
  1.9 0.0 copy-done.1
  1.9 0.0 copy-done.2
  1.9 64.9 %shard_map.67 = (f32[2,16,512]{2,1,0:T(8,128)S(1)}, f32[64,256]{1,0:T(8,128)S(1)}, f32[2,256,256]{2,1,0:T(8,128)S(1)}) custom-call(bf16[2,512,256]{2,1,0:T(8,128)(2,1)S(1)} %bitcast.15, bf16[2,2,256,256]{3,2,1,0:T(8,128)(2,1)S(1)} %copy-done, bf16[2,256,256]{2,1,0:T(8,128)(2,1)S(1)} %bitcast.17, bf16[2,16,512]{2,1,0:T(8,128)(2,1)S(1)} %bitcast.20), custom_call_target="tpu_custom_call" | custom-call | tf_op jit(solution)/shard_map/pallas_call | solution.py:382
  66.8 0.6 copy.15
  67.5 0.6 copy.16
  68.1 0.8 %copy.17 = f32[2,1,256,256]{3,2,1,0:T(8,128)} copy(f32[2,1,256,256]{3,2,1,0:T(8,128)S(1)} %bitcast.16) | data formatting | bytes 1048576
Async XLA Ops:
  0.6 1.2 %copy-start = (bf16[2,2,256,256]{3,2,1,0:T(8,128)(2,1)S(1)}, bf16[2,2,256,256]{3,2,1,0:T(8,128)(2,1)}, u32[]{:S(2)}) copy-start(bf16[2,2,256,256]{3,2,1,0:T(8,128)(2,1)} %ws_ref.1) | copy-start | bytes 1572868
  0.6 1.3 %copy-start.1 = (bf16[2,1,256,256]{3,2,1,0:T(8,128)(2,1)S(1)}, bf16[2,1,256,256]{3,2,1,0:T(8,128)(2,1)}, u32[]{:S(2)}) copy-start(bf16[2,1,256,256]{3,2,1,0:T(8,128)(2,1)} %param.6) | copy-start | bytes 786436
  0.7 1.2 %copy-start.2 = (bf16[2,1,16,512]{3,2,1,0:T(8,128)(2,1)S(1)}, bf16[2,1,16,512]{3,2,1,0:T(8,128)(2,1)}, u32[]{:S(2)}) copy-start(bf16[2,1,16,512]{3,2,1,0:T(8,128)(2,1)} %param.7) | copy-start | bytes 98308

commit v4 on v3

--- a/solution.py
+++ b/solution.py
@@ -11,7 +11,8 @@
 MESH = pl.DeviceIdType.MESH
 CUTS = 16
 
-(COT, GEX, RS1, RS2, AG1, AG2, TEX, AMP, ZS2, ZS1, N3A, N3B, F3, B3, NS, FS, BS, PHASES) = range(18)
+(COT, GEX, RS1, RS2, AG1, AG2, TEX, ZS2, ZS1, NS, FS, BS, N3, F3, B3) = range(15)
+PHASES = 18
 
 LINE = sorted(range(1, 16), key=lambda n: -min(n, 16 - n))
 NEAR = [(2, 1), (2, 0), (-1, 1), (1, 1), (-1, 0), (1, 0), (0, 1)]
@@ -49,7 +50,7 @@
 
 def kernel(b_ref, ws_ref, w3_ref, cot_ref, amp_ref, gs_ref, gl_ref,
            bp, fst, xdc, xp, xnat, w3p, cotr, gcat, grot, gsend, grecv, gown,
-           tbuf, trecv, sbuf, recv2, gt, tsend, texr, asend, arecv, bk, b1p,
+           tbuf, trecv, sbuf, recv2, gt, tsend, texr, bk, b1p,
            z1s, z1r, z2s, z2r, zs3, nr3, clsx, cls3, zfin,
            ss, nrs, fx, sfin, send_sem, recv_sem):
     cid = lax.axis_index("cuts")
@@ -61,10 +62,12 @@
 
     totals = {
         COT: cotr.at[pl.ds(0, 15)], GEX: grecv.at[pl.ds(0, 15)], RS1: trecv, RS2: recv2.at[pl.ds(0, 15)],
-        AG1: gt.at[0, pl.ds(0, 15)], AG2: gt.at[0], TEX: texr.at[pl.ds(0, 15)], AMP: arecv.at[pl.ds(0, 15)],
-        ZS2: z2r.at[pl.ds(0, 15)], ZS1: z1r.at[pl.ds(0, 15)], N3A: nr3.at[0, pl.ds(0, 7)],
-        N3B: nr3.at[0, pl.ds(0, 7)], F3: clsx.at[pl.ds(0, 3)], B3: zfin.at[pl.ds(0, 7)],
-        NS: nrs.at[pl.ds(0, 7)], FS: fx.at[pl.ds(0, 3)], BS: sfin.at[pl.ds(0, 7)]}
+        AG1: gt.at[0, pl.ds(0, 15)], AG2: gt.at[0], TEX: texr.at[pl.ds(0, 15)],
+        ZS2: z2r.at[pl.ds(0, 15)], ZS1: z1r.at[pl.ds(0, 15)], NS: nrs.at[pl.ds(0, 7)], FS: fx.at[pl.ds(0, 3)], BS: sfin.at[pl.ds(0, 7)]}
+    for part in (0, 3):
+        totals[N3 + part] = nr3.at[0, pl.ds(0, 7)]
+        totals[F3 + part] = clsx.at[0, pl.ds(0, 3)]
+        totals[B3 + part] = zfin.at[0, pl.ds(0, 7)]
     started = []
 
     def push(phase, src, dst, cuts=None, idx=None):
@@ -204,6 +207,50 @@
             to = 2 * chip_at(dy, dx) + (core ^ dc)
             push(phase, src.at[to], dst.at[cid], cuts=to)
         dst[cid] = src[cid]
+
+    def near(phase, src, dst):
+        for step, flip in NEAR:
+            to_z, to_x = (z + step) & 15, xl ^ flip
+            push(phase, src.at[((to_z & 3) << 1) + to_x], dst.at[2 * (step + 1) + flip], idx=2 * to_z + to_x)
+        dst[2] = src[cls]
+
+    def near_back(phase, src, dst):
+        for step, flip in NEAR:
+            push(phase, src, dst.at[cls], idx=2 * ((z - step) & 15) + (xl ^ flip))
+
+    def add_up(ref, count):
+        out = ref[0].astype(F32)
+        for n in range(1, count):
+            out = out + ref[n].astype(F32)
+        return out
+
+    def push_far(phase, ref):
+        for hop in (2, 1, 3):
+            push(phase, ref.at[far], ref.at[far], idx=2 * (4 * ((far + hop) & 3) + (z & 3)) + xl)
+
+    def grad_three(half, part):
+        g = [jnp.concatenate([jnp.concatenate([gt[half, 2 * n, p], gt[half, 2 * n + 1, p]], axis=1)
+                              for n in range(8)], axis=0) for p in range(2)]
+        z_re = dot(xnat[0], g[0], (1, 1)) + dot(xnat[1], g[1], (1, 1))
+        z_im = dot(xnat[0], g[1], (1, 1)) - dot(xnat[1], g[0], (1, 1))
+        zs3[half, 0:4] = z_re.astype(BF).reshape(4, 64, 128)
+        zs3[half, 4:8] = z_im.astype(BF).reshape(4, 64, 128)
+        near(N3 + part, zs3.at[half], nr3.at[half])
+
+    def sum_three(half, part):
+        arrived(N3 + part)
+        clsx[half, far] = add_up(nr3.at[half], 8).astype(BF)
+        push_far(F3 + part, clsx.at[half])
+
+    def spread_three(half, part):
+        arrived(F3 + part)
+        cls3[half] = add_up(clsx.at[half], 4).astype(BF)
+        near_back(B3 + part, cls3.at[half], zfin.at[half])
+        zfin[half, cls] = cls3[half]
+
+    arrived(AG1)
+    push(AG2, gt.at[core], gt.at[core], cuts=cid ^ 1)
+    grad_three(core, 0)
 
     arrived(TEX)
     t_all = texr[...].astype(F32).reshape(16, 2, 8, 128)
@@ -227,42 +274,20 @@
     t_cat = dot(to_u, jnp.concatenate(cat, axis=0)).astype(BF)
     t_rot = dot(to_u, jnp.concatenate(rot, axis=0)).astype(BF)
     amp = dot(ws_ref[1, 0], t_cat, (0, 0)) + dot(ws_ref[1, 1], t_rot, (0, 0))
-    asend[...] = amp.reshape(CUTS, 16, 128)
-    z2s[:, 0] = dot(t_cat, gcat[...], (1, 1)).astype(BF).reshape(CUTS, 16, 256)
-    z2s[:, 1] = dot(t_cat, grot[...], (1, 1)).astype(BF).reshape(CUTS, 16, 256)
+    low = pltpu.roll(amp - amp.astype(BF).astype(F32), 64, 1)
+    amp = jnp.where(lax.broadcasted_iota(jnp.int32, (256, 128), 1) < 64, amp, low)
+    z2s[:, :, 0:128] = amp.astype(BF).reshape(CUTS, 16, 128)
+    z2s[:, :, 128:384] = dot(t_cat, gcat[...], (1, 1)).astype(BF).reshape(CUTS, 16, 256)
+    z2s[:, :, 384:640] = dot(t_cat, grot[...], (1, 1)).astype(BF).reshape(CUTS, 16, 256)
     push_cuts(ZS2, z2s, z2r)
-    push_cuts(AMP, asend, arecv)
-
-    def near(phase, src, dst):
-        for step, flip in NEAR:
-            to_z, to_x = (z + step) & 15, xl ^ flip
-            push(phase, src.at[((to_z & 3) << 1) + to_x], dst.at[2 * (step + 1) + flip], idx=2 * to_z + to_x)
-        dst[2] = src[cls]
-
-    def near_back(phase, src, dst):
-        for step, flip in NEAR:
-            push(phase, src, dst.at[cls], idx=2 * ((z - step) & 15) + (xl ^ flip))
-
-    def grad_three(half, phase):
-        g = [jnp.concatenate([jnp.concatenate([gt[half, 2 * n, p], gt[half, 2 * n + 1, p]], axis=1)
-                              for n in range(8)], axis=0) for p in range(2)]
-        z_re = dot(xnat[0], g[0], (1, 1)) + dot(xnat[1], g[1], (1, 1))
-        z_im = dot(xnat[0], g[1], (1, 1)) - dot(xnat[1], g[0], (1, 1))
-        zs3[half, 0:4] = z_re.astype(BF).reshape(4, 64, 128)
-        zs3[half, 4:8] = z_im.astype(BF).reshape(4, 64, 128)
-        near(phase, zs3.at[half], nr3.at[half])
-
-    arrived(AG1)
-    push(AG2, gt.at[core], gt.at[core], cuts=cid ^ 1)
-    grad_three(core, N3A)
+
     arrived(AG2)
-    grad_three(1 - core, N3B)
-
     gr, gi = [
-        dot(jnp.concatenate([jnp.concatenate([gt[c & 1, 2 * (c >> 1), p], gt[c & 1, 2 * (c >> 1) + 1, p]], axis=1)
-                             for c in range(CUTS)], axis=0), to_xlkz, (1, 1)).astype(BF) for p in range(2)]
-    bk[0] = dot(w3p[0], gr) + dot(w3p[1], gi)
-    bk[1] = dot(w3p[0], gi) - dot(w3p[1], gr)
+        jnp.concatenate([jnp.concatenate([gt[c & 1, 2 * (c >> 1), p], gt[c & 1, 2 * (c >> 1) + 1, p]], axis=1)
+                         for c in range(CUTS)], axis=0) for p in range(2)]
+    nr, ni = [dot(g, to_xlkz, (1, 1)).astype(BF) for g in (gr, gi)]
+    bk[0] = dot(w3p[0], nr) + dot(w3p[1], ni)
+    bk[1] = dot(w3p[0], ni) - dot(w3p[1], nr)
     for p in range(2):
         for uk in range(16):
             for g in range(2):
@@ -275,50 +300,41 @@
     z1s[:, 1] = dot(z_im.astype(BF), to_dc).astype(BF).reshape(CUTS, 16, 256)
     push_cuts(ZS1, z1s, z1r)
 
-    def add_up(ref, count):
-        out = ref[0].astype(F32)
-        for n in range(1, count):
-            out = out + ref[n].astype(F32)
-        return out
-
-    def push_far(phase, ref):
-        for hop in (2, 1, 3):
-            push(phase, ref.at[far], ref.at[far], idx=2 * (4 * ((far + hop) & 3) + (z & 3)) + xl)
-
-    arrived(N3A)
-    arrived(N3B)
-    for half in range(2):
-        clsx[far, half] = add_up(nr3.at[half], 8).astype(BF)
-    push_far(F3, clsx)
+    grad_three(1 - core, 3)
+
+    sum_three(core, 0)
+    sum_three(1 - core, 3)
 
     arrived(ZS2)
-    ss[4:8] = add_up(z2r, CUTS).reshape(4, 8, 256)
+    part = z2r[0].astype(F32)
+    for n in range(1, CUTS):
+        part = part + z2r[n].astype(F32)
+    for p in range(2):
+        ss[4 + 2 * p:6 + 2 * p] = part[:, 128 + 256 * p:384 + 256 * p].reshape(2, 8, 256)
+
     arrived(ZS1)
     ss[0:4] = add_up(z1r, CUTS).reshape(4, 8, 256)
     near(NS, ss, nrs)
 
-    arrived(F3)
-    cls3[...] = add_up(clsx, 4).astype(BF)
-    near_back(B3, cls3, zfin)
-    zfin[cls] = cls3[...]
+    spread_three(core, 0)
+
+    group = lax.broadcasted_iota(jnp.int32, (16, 128), 1) >> 5
+    for g in range(4):
+        blocks = [z2r[4 * g + j, :, 0:128].astype(F32) for j in range(4)]
+        blocks = [b + pltpu.roll(b, 64, 1) for b in blocks]
+        for p in range(2):
+            out = None
+            for j in range(4):
+                shift = (32 * j - 32 * p) % 128
+                moved = pltpu.roll(blocks[j], shift, 1) if shift else blocks[j]
+                out = moved if out is None else jnp.where(group == j, moved, out)
+            amp_ref[p, :, 128 * g:128 * g + 128] = out
 
     arrived(NS)
     fx[far] = add_up(nrs, 8)
     push_far(FS, fx)
 
-    arrived(AMP)
-    group = lax.broadcasted_iota(jnp.int32, (8, 128), 1) >> 5
-    for p in range(2):
-        for g in range(4):
-            for h in range(2):
-                rows = slice(8 * h, 8 * h + 8)
-                out = None
-                for j in range(4):
-                    block = arecv[4 * g + j, rows]
-                    shift = (32 * j - 32 * p) % 128
-                    moved = pltpu.roll(block, shift, 1) if shift else block
-                    out = moved if out is None else jnp.where(group == j, moved, out)
-                amp_ref[p, rows, 128 * g:128 * g + 128] = out
+    spread_three(1 - core, 3)
 
     arrived(FS)
     sfin[cls] = add_up(fx, 4)
@@ -327,8 +343,9 @@
     to_cut = selection(256, 256, lambda r, c: ((r >> 7) == ((c >> 4) & 1)) & (((r >> 4) & 7) == (c >> 5))
                        & ((r & 15) == (c & 15)))
     arrived(B3)
+    arrived(B3 + 3)
     for n in range(8):
-        block = jnp.concatenate([zfin[n, 0], zfin[n, 1]], axis=1)
+        block = jnp.concatenate([zfin[0, n], zfin[1, n]], axis=1)
         gl_ref[n // 4, 64 * (n % 4):64 * (n % 4) + 64] = dot(block, to_cut)
     arrived(BS)
     gs_ref[...] = sfin[...].reshape(64, 256)
@@ -359,19 +376,17 @@
         vmem((2, 16, 2, 16, 256), BF),
         vmem((16, 16, 128), BF),
         vmem((16, 16, 128), BF),
-        vmem((CUTS, 16, 128), F32),
-        vmem((CUTS, 16, 128), F32),
         vmem((2, 256, 512), F32),
         vmem((2, 512, 256), BF),
         vmem((CUTS, 2, 16, 256), BF),
         vmem((CUTS, 2, 16, 256), BF),
-        vmem((CUTS, 2, 16, 256), BF),
-        vmem((CUTS, 2, 16, 256), BF),
+        vmem((CUTS, 16, 640), BF),
+        vmem((CUTS, 16, 640), BF),
         vmem((2, 8, 64, 128), BF),
         vmem((2, 8, 64, 128), BF),
-        vmem((4, 2, 64, 128), BF),
+        vmem((2, 4, 64, 128), BF),
         vmem((2, 64, 128), BF),
-        vmem((8, 2, 64, 128), BF),
+        vmem((2, 8, 64, 128), BF),
         vmem((8, 8, 256), F32),
         vmem((8, 8, 256), F32),
         vmem((4, 8, 256), F32),

time: 69 us -> 65.7 us (0.952)
  the two profiles are of different devices: /device:TPU:4 before, /device:TPU:2 now
where the time goes in v4:
time: 65.7 us; the launch traced here: 65.5 us
  Pallas kernels  61.6 us (94%)
  local copies, waits for them, and re-layouts  3.29 us (5%)
  between operations  0.68 us (1%)
    pallas_call x1, Pallas kernels, local(): pl.pallas_call(kernel, out_shape=(jax.ShapeDtypeStruct((2, 16, 512), F32)...  61.6 us
    unnamed x10, local copies, waits for them, and re-layouts  3.29 us

profile of v4, /device:TPU:2, one launch (start us, length us, event | category | flops | bytes accessed | tf_op | source)
XLA Modules:
  0.0 65.5 jit_solution(2049814605152197430)
XLA Ops:
  0.6 0.0 copy-start
  0.6 0.0 copy-start.1
  0.7 0.0 copy-start.2
  0.7 1.2 %copy.11 = bf16[1,2,512,256]{3,2,1,0:T(8,128)(2,1)S(1)} copy(bf16[1,2,512,256]{3,1,2,0:T(2,128)(2,1)} %bitcast.21) | data formatting | bytes 1048576
  1.8 0.0 copy-done
  1.9 0.0 copy-done.1
  1.9 0.0 copy-done.2
  1.9 61.6 %shard_map.67 = (f32[2,16,512]{2,1,0:T(8,128)S(1)}, f32[64,256]{1,0:T(8,128)S(1)}, f32[2,256,256]{2,1,0:T(8,128)S(1)}) custom-call(bf16[2,512,256]{2,1,0:T(8,128)(2,1)S(1)} %bitcast.15, bf16[2,2,256,256]{3,2,1,0:T(8,128)(2,1)S(1)} %copy-done, bf16[2,256,256]{2,1,0:T(8,128)(2,1)S(1)} %bitcast.17, bf16[2,16,512]{2,1,0:T(8,128)(2,1)S(1)} %bitcast.20), custom_call_target="tpu_custom_call" | custom-call | tf_op jit(solution)/shard_map/pallas_call | solution.py:397
  63.5 0.6 copy.15
  64.1 0.6 copy.16
  64.7 0.8 %copy.17 = f32[2,1,256,256]{3,2,1,0:T(8,128)} copy(f32[2,1,256,256]{3,2,1,0:T(8,128)S(1)} %bitcast.16) | data formatting | bytes 1048576
Async XLA Ops:
  0.6 1.2 %copy-start = (bf16[2,2,256,256]{3,2,1,0:T(8,128)(2,1)S(1)}, bf16[2,2,256,256]{3,2,1,0:T(8,128)(2,1)}, u32[]{:S(2)}) copy-start(bf16[2,2,256,256]{3,2,1,0:T(8,128)(2,1)} %ws_ref.1) | copy-start | bytes 1572868
  0.6 1.3 %copy-start.1 = (bf16[2,1,256,256]{3,2,1,0:T(8,128)(2,1)S(1)}, bf16[2,1,256,256]{3,2,1,0:T(8,128)(2,1)}, u32[]{:S(2)}) copy-start(bf16[2,1,256,256]{3,2,1,0:T(8,128)(2,1)} %param.6) | copy-start | bytes 786436
  0.7 1.2 %copy-start.2 = (bf16[2,1,16,512]{3,2,1,0:T(8,128)(2,1)S(1)}, bf16[2,1,16,512]{3,2,1,0:T(8,128)(2,1)}, u32[]{:S(2)}) copy-start(bf16[2,1,16,512]{3,2,1,0:T(8,128)(2,1)} %param.7) | copy-start | bytes 98308

commit v5 on v4

--- a/solution.py
+++ b/solution.py
@@ -48,10 +48,10 @@
     return out
 
 
-def kernel(b_ref, ws_ref, w3_ref, cot_ref, amp_ref, gs_ref, gl_ref,
+def kernel(b_ref, ws_ref, w3_ref, cot_ref, amp_ref, gs_ref, zfin,
            bp, fst, xdc, xp, xnat, w3p, cotr, gcat, grot, gsend, grecv, gown,
            tbuf, trecv, sbuf, recv2, gt, tsend, texr, bk, b1p,
-           z1s, z1r, z2s, z2r, zs3, nr3, clsx, cls3, zfin,
+           z1s, z1r, z2s, z2r, zs3, nr3, clsx, cls3,
            ss, nrs, fx, sfin, send_sem, recv_sem):
     cid = lax.axis_index("cuts")
     iid = lax.axis_index("idx")
@@ -316,8 +316,6 @@
     ss[0:4] = add_up(z1r, CUTS).reshape(4, 8, 256)
     near(NS, ss, nrs)
 
-    spread_three(core, 0)
-
     group = lax.broadcasted_iota(jnp.int32, (16, 128), 1) >> 5
     for g in range(4):
         blocks = [z2r[4 * g + j, :, 0:128].astype(F32) for j in range(4)]
@@ -334,24 +332,36 @@
     fx[far] = add_up(nrs, 8)
     push_far(FS, fx)
 
+    spread_three(core, 0)
     spread_three(1 - core, 3)
 
     arrived(FS)
     sfin[cls] = add_up(fx, 4)
     near_back(BS, sfin.at[cls], sfin)
 
+    arrived(B3)
+    arrived(B3 + 3)
+    arrived(BS)
+    gs_ref[...] = sfin[...].reshape(64, 256)
+
+    for phase in started:
+        pltpu.make_async_copy(totals[phase], totals[phase], send_sem.at[phase]).wait()
+
+
+def results(amp_ref, gs_ref, zfin, amp_hbm, gs_hbm, gl_hbm, stage, sem):
+    stores = [pltpu.make_async_copy(amp_ref, amp_hbm, sem.at[0]), pltpu.make_async_copy(gs_ref, gs_hbm, sem.at[1])]
+    for store in stores:
+        store.start()
     to_cut = selection(256, 256, lambda r, c: ((r >> 7) == ((c >> 4) & 1)) & (((r >> 4) & 7) == (c >> 5))
                        & ((r & 15) == (c & 15)))
-    arrived(B3)
-    arrived(B3 + 3)
-    for n in range(8):
-        block = jnp.concatenate([zfin[0, n], zfin[1, n]], axis=1)
-        gl_ref[n // 4, 64 * (n % 4):64 * (n % 4) + 64] = dot(block, to_cut)
-    arrived(BS)
-    gs_ref[...] = sfin[...].reshape(64, 256)
-
-    for phase in started:
-        pltpu.make_async_copy(totals[phase], totals[phase], send_sem.at[phase]).wait()
+    for p in range(2):
+        for n in range(4):
+            block = jnp.concatenate([zfin[0, 4 * p + n], zfin[1, 4 * p + n]], axis=1)
+            stage[p, 64 * n:64 * n + 64] = dot(block, to_cut)
+        stores.append(pltpu.make_async_copy(stage.at[p], gl_hbm.at[p], sem.at[2 + p]))
+        stores[-1].start()
+    for store in stores:
+        store.wait()
 
 
 def local(boundary, gates_shared, gates_sliced, cotangent):
@@ -386,7 +396,6 @@
         vmem((2, 8, 64, 128), BF),
         vmem((2, 4, 64, 128), BF),
         vmem((2, 64, 128), BF),
-        vmem((2, 8, 64, 128), BF),
         vmem((8, 8, 256), F32),
         vmem((8, 8, 256), F32),
         vmem((4, 8, 256), F32),
@@ -394,19 +403,33 @@
         pltpu.SemaphoreType.DMA((PHASES,)),
         pltpu.SemaphoreType.DMA((PHASES,)),
     ]
+    hbm = pl.BlockSpec(memory_space=pltpu.HBM)
+    whole = pl.BlockSpec(memory_space=vmem)
+    parts = pl.pallas_call(
+        kernel,
+        out_shape=(
+            jax.ShapeDtypeStruct((2, 16, 512), F32),
+            jax.ShapeDtypeStruct((64, 256), F32),
+            jax.ShapeDtypeStruct((2, 8, 64, 128), BF),
+        ),
+        in_specs=[whole] * 4,
+        out_specs=[whole] * 3,
+        scratch_shapes=scratch,
+        compiler_params=pltpu.CompilerParams(
+            collective_id=0, has_side_effects=True, vmem_limit_bytes=40 * 2 ** 20),
+    )(boundary.reshape(2, 512, 256), gates_shared, gates_sliced[:, 0], cotangent[:, 0])
     amp, shared, sliced = pl.pallas_call(
-        kernel,
+        results,
         out_shape=(
             jax.ShapeDtypeStruct((2, 16, 512), F32),
             jax.ShapeDtypeStruct((64, 256), F32),
             jax.ShapeDtypeStruct((2, 256, 256), F32),
         ),
-        in_specs=[pl.BlockSpec(memory_space=vmem)] * 4,
-        out_specs=[pl.BlockSpec(memory_space=vmem)] * 3,
-        scratch_shapes=scratch,
-        compiler_params=pltpu.CompilerParams(
-            collective_id=0, has_side_effects=True, vmem_limit_bytes=40 * 2 ** 20),
-    )(boundary.reshape(2, 512, 256), gates_shared, gates_sliced[:, 0], cotangent[:, 0])
+        in_specs=[whole] * 3,
+        out_specs=[hbm] * 3,
+        scratch_shapes=[vmem((2, 256, 256), F32), pltpu.SemaphoreType.DMA((4,))],
+        compiler_params=pltpu.CompilerParams(vmem_limit_bytes=8 * 2 ** 20),
+    )(*parts)
     return amp[:, None], shared.reshape(2, 2, 16, 256), sliced[:, None]
 
 

time: 65.7 us -> 64.5 us (0.982)
  local copies, waits for them, and re-layouts: 3.29 us -> 1.23 us
  Pallas kernels: 61.6 us -> 62.5 us
    unnamed x10 -> x7, local copies, waits for them, and re-layouts: 3.29 us -> 1.23 us
    pallas_call x0 -> x1, Pallas kernels: none -> 1.08 us  [local(): pl.pallas_call(results, out_shape=(jax.ShapeDtypeStruct((2, 16, 512), F32...]
where the time goes in v5:
time: 64.5 us; the launch traced here: 64.4 us
  Pallas kernels  62.5 us (97%)
  local copies, waits for them, and re-layouts  1.23 us (2%)
  between operations  0.67 us (1%)
    pallas_call x1, Pallas kernels, local(): pl.pallas_call(kernel, out_shape=(jax.ShapeDtypeStruct((2, 16, 512), F32)...  61.4 us

profile of v5, /device:TPU:2, one launch (start us, length us, event | category | flops | bytes accessed | tf_op | source)
XLA Modules:
  0.0 64.4 jit_solution(2152413321793222408)
XLA Ops:
  0.6 0.0 copy-start
  0.6 0.0 copy-start.1
  0.7 0.0 copy-start.2
  0.7 1.2 %copy.11 = bf16[1,2,512,256]{3,2,1,0:T(8,128)(2,1)S(1)} copy(bf16[1,2,512,256]{3,1,2,0:T(2,128)(2,1)} %bitcast.18) | data formatting | bytes 1048576
  1.8 0.0 copy-done
  1.9 0.0 copy-done.1
  1.9 0.0 copy-done.2
  1.9 61.4 %shard_map.67 = (f32[2,16,512]{2,1,0:T(8,128)S(1)}, f32[64,256]{1,0:T(8,128)S(1)}, bf16[2,8,64,128]{3,2,1,0:T(8,128)(2,1)S(1)}) custom-call(bf16[2,512,256]{2,1,0:T(8,128)(2,1)S(1)} %bitcast.15, bf16[2,2,256,256]{3,2,1,0:T(8,128)(2,1)S(1)} %copy-done, bf16[2,256,256]{2,1,0:T(8,128)(2,1)S(1)} %bitcast.16, bf16[2,16,512]{2,1,0:T(8,128)(2,1)S(1)} %bitcast.17), custom_call_target="tpu_custom_call" | custom-call | tf_op jit(solution)/shard_map/pallas_call | solution.py:408
  63.3 1.1 %shard_map.68 = (f32[2,16,512]{2,1,0:T(8,128)}, f32[64,256]{1,0:T(8,128)}, f32[2,256,256]{2,1,0:T(8,128)}) custom-call(f32[2,16,512]{2,1,0:T(8,128)S(1)} %get-tuple-element.9.amp_ref, f32[64,256]{1,0:T(8,128)S(1)} %get-tuple-element.10.gs_ref, bf16[2,8,64,128]{3,2,1,0:T(8,128)(2,1)S(1)} %get-tuple-element.11.zfin), custom_call_target="tpu_custom_call" | custom-call | tf_op jit(solution)/shard_map/pallas_call | solution.py:421
Async XLA Ops:
  0.6 1.2 %copy-start = (bf16[2,2,256,256]{3,2,1,0:T(8,128)(2,1)S(1)}, bf16[2,2,256,256]{3,2,1,0:T(8,128)(2,1)}, u32[]{:S(2)}) copy-start(bf16[2,2,256,256]{3,2,1,0:T(8,128)(2,1)} %ws_ref.1) | copy-start | bytes 1572868
  0.6 1.3 %copy-start.1 = (bf16[2,1,256,256]{3,2,1,0:T(8,128)(2,1)S(1)}, bf16[2,1,256,256]{3,2,1,0:T(8,128)(2,1)}, u32[]{:S(2)}) copy-start(bf16[2,1,256,256]{3,2,1,0:T(8,128)(2,1)} %param.6) | copy-start | bytes 786436
  0.7 1.2 %copy-start.2 = (bf16[2,1,16,512]{3,2,1,0:T(8,128)(2,1)S(1)}, bf16[2,1,16,512]{3,2,1,0:T(8,128)(2,1)}, u32[]{:S(2)}) copy-start(bf16[2,1,16,512]{3,2,1,0:T(8,128)(2,1)} %param.7) | copy-start | bytes 98308

commit v6 on v5

--- a/solution.py
+++ b/solution.py
@@ -48,10 +48,10 @@
     return out
 
 
-def kernel(b_ref, ws_ref, w3_ref, cot_ref, amp_ref, gs_ref, zfin,
+def kernel(b_ref, ws_ref, w3_ref, cot_ref, amp_ref, gs_ref, gl_ref,
            bp, fst, xdc, xp, xnat, w3p, cotr, gcat, grot, gsend, grecv, gown,
            tbuf, trecv, sbuf, recv2, gt, tsend, texr, bk, b1p,
-           z1s, z1r, z2s, z2r, zs3, nr3, clsx, cls3,
+           z1s, z1r, z2s, z2r, zs3, nr3, clsx, cls3, zfin,
            ss, nrs, fx, sfin, send_sem, recv_sem):
     cid = lax.axis_index("cuts")
     iid = lax.axis_index("idx")
@@ -282,6 +282,7 @@
     push_cuts(ZS2, z2s, z2r)
 
     arrived(AG2)
+    grad_three(1 - core, 3)
     gr, gi = [
         jnp.concatenate([jnp.concatenate([gt[c & 1, 2 * (c >> 1), p], gt[c & 1, 2 * (c >> 1) + 1, p]], axis=1)
                          for c in range(CUTS)], axis=0) for p in range(2)]
@@ -299,8 +300,6 @@
     z1s[:, 0] = dot(z_re.astype(BF), to_dc).astype(BF).reshape(CUTS, 16, 256)
     z1s[:, 1] = dot(z_im.astype(BF), to_dc).astype(BF).reshape(CUTS, 16, 256)
     push_cuts(ZS1, z1s, z1r)
-
-    grad_three(1 - core, 3)
 
     sum_three(core, 0)
     sum_three(1 - core, 3)
@@ -341,6 +340,11 @@
 
     arrived(B3)
     arrived(B3 + 3)
+    to_cut = selection(256, 256, lambda r, c: ((r >> 7) == ((c >> 4) & 1)) & (((r >> 4) & 7) == (c >> 5))
+                       & ((r & 15) == (c & 15)))
+    for n in range(8):
+        block = jnp.concatenate([zfin[0, n], zfin[1, n]], axis=1)
+        gl_ref[n // 4, 64 * (n % 4):64 * (n % 4) + 64] = dot(block, to_cut)
     arrived(BS)
     gs_ref[...] = sfin[...].reshape(64, 256)
 
@@ -348,18 +352,11 @@
         pltpu.make_async_copy(totals[phase], totals[phase], send_sem.at[phase]).wait()
 
 
-def results(amp_ref, gs_ref, zfin, amp_hbm, gs_hbm, gl_hbm, stage, sem):
-    stores = [pltpu.make_async_copy(amp_ref, amp_hbm, sem.at[0]), pltpu.make_async_copy(gs_ref, gs_hbm, sem.at[1])]
+def results(amp_ref, gs_ref, gl_ref, amp_hbm, gs_hbm, gl_hbm, sem):
+    stores = [pltpu.make_async_copy(src, dst, sem.at[n]) for n, (src, dst) in enumerate(
+        ((gl_ref, gl_hbm), (amp_ref, amp_hbm), (gs_ref, gs_hbm)))]
     for store in stores:
         store.start()
-    to_cut = selection(256, 256, lambda r, c: ((r >> 7) == ((c >> 4) & 1)) & (((r >> 4) & 7) == (c >> 5))
-                       & ((r & 15) == (c & 15)))
-    for p in range(2):
-        for n in range(4):
-            block = jnp.concatenate([zfin[0, 4 * p + n], zfin[1, 4 * p + n]], axis=1)
-            stage[p, 64 * n:64 * n + 64] = dot(block, to_cut)
-        stores.append(pltpu.make_async_copy(stage.at[p], gl_hbm.at[p], sem.at[2 + p]))
-        stores[-1].start()
     for store in stores:
         store.wait()
 
@@ -396,6 +393,7 @@
         vmem((2, 8, 64, 128), BF),
         vmem((2, 4, 64, 128), BF),
         vmem((2, 64, 128), BF),
+        vmem((2, 8, 64, 128), BF),
         vmem((8, 8, 256), F32),
         vmem((8, 8, 256), F32),
         vmem((4, 8, 256), F32),
@@ -410,7 +408,7 @@
         out_shape=(
             jax.ShapeDtypeStruct((2, 16, 512), F32),
             jax.ShapeDtypeStruct((64, 256), F32),
-            jax.ShapeDtypeStruct((2, 8, 64, 128), BF),
+            jax.ShapeDtypeStruct((2, 256, 256), F32),
         ),
         in_specs=[whole] * 4,
         out_specs=[whole] * 3,
@@ -427,7 +425,7 @@
         ),
         in_specs=[whole] * 3,
         out_specs=[hbm] * 3,
-        scratch_shapes=[vmem((2, 256, 256), F32), pltpu.SemaphoreType.DMA((4,))],
+        scratch_shapes=[pltpu.SemaphoreType.DMA((3,))],
         compiler_params=pltpu.CompilerParams(vmem_limit_bytes=8 * 2 ** 20),
     )(*parts)
     return amp[:, None], shared.reshape(2, 2, 16, 256), sliced[:, None]

time: 64.5 us -> 64.3 us (level)
  no operation moved by 1% of the time
where the time goes in v6:
time: 64.3 us; the launch traced here: 64.2 us
  Pallas kernels  62.3 us (97%)
  local copies, waits for them, and re-layouts  1.23 us (2%)
  between operations  0.67 us (1%)
    pallas_call x1, Pallas kernels, local(): pl.pallas_call(kernel, out_shape=(jax.ShapeDtypeStruct((2, 16, 512), F32)...  61.4 us

profile of v6, /device:TPU:2, one launch (start us, length us, event | category | flops | bytes accessed | tf_op | source)
XLA Modules:
  0.0 64.2 jit_solution(6757770801857222231)
XLA Ops:
  0.6 0.0 copy-start
  0.6 0.0 copy-start.1
  0.7 0.0 copy-start.2
  0.7 1.2 %copy.11 = bf16[1,2,512,256]{3,2,1,0:T(8,128)(2,1)S(1)} copy(bf16[1,2,512,256]{3,1,2,0:T(2,128)(2,1)} %bitcast.18) | data formatting | bytes 1048576
  1.8 0.0 copy-done
  1.9 0.0 copy-done.1
  1.9 0.0 copy-done.2
  1.9 61.4 %shard_map.67 = (f32[2,16,512]{2,1,0:T(8,128)S(1)}, f32[64,256]{1,0:T(8,128)S(1)}, f32[2,256,256]{2,1,0:T(8,128)S(1)}) custom-call(bf16[2,512,256]{2,1,0:T(8,128)(2,1)S(1)} %bitcast.15, bf16[2,2,256,256]{3,2,1,0:T(8,128)(2,1)S(1)} %copy-done, bf16[2,256,256]{2,1,0:T(8,128)(2,1)S(1)} %bitcast.16, bf16[2,16,512]{2,1,0:T(8,128)(2,1)S(1)} %bitcast.17), custom_call_target="tpu_custom_call" | custom-call | tf_op jit(solution)/shard_map/pallas_call | solution.py:406
  63.3 0.9 %shard_map.68 = (f32[2,16,512]{2,1,0:T(8,128)}, f32[64,256]{1,0:T(8,128)}, f32[2,256,256]{2,1,0:T(8,128)}) custom-call(f32[2,16,512]{2,1,0:T(8,128)S(1)} %get-tuple-element.9.amp_ref, f32[64,256]{1,0:T(8,128)S(1)} %get-tuple-element.10.gs_ref, f32[2,256,256]{2,1,0:T(8,128)S(1)} %get-tuple-element.11.gl_ref), custom_call_target="tpu_custom_call" | custom-call | tf_op jit(solution)/shard_map/pallas_call | solution.py:419
Async XLA Ops:
  0.6 1.2 %copy-start = (bf16[2,2,256,256]{3,2,1,0:T(8,128)(2,1)S(1)}, bf16[2,2,256,256]{3,2,1,0:T(8,128)(2,1)}, u32[]{:S(2)}) copy-start(bf16[2,2,256,256]{3,2,1,0:T(8,128)(2,1)} %ws_ref.1) | copy-start | bytes 1572868
  0.6 1.3 %copy-start.1 = (bf16[2,1,256,256]{3,2,1,0:T(8,128)(2,1)S(1)}, bf16[2,1,256,256]{3,2,1,0:T(8,128)(2,1)}, u32[]{:S(2)}) copy-start(bf16[2,1,256,256]{3,2,1,0:T(8,128)(2,1)} %param.6) | copy-start | bytes 786436
  0.7 1.2 %copy-start.2 = (bf16[2,1,16,512]{3,2,1,0:T(8,128)(2,1)S(1)}, bf16[2,1,16,512]{3,2,1,0:T(8,128)(2,1)}, u32[]{:S(2)}) copy-start(bf16[2,1,16,512]{3,2,1,0:T(8,128)(2,1)} %param.7) | copy-start | bytes 98308
